TPU v7x, 512 devices: a whole 4x8x8 slice. The times are simulated.
512 devices in a mesh: dp: 32 (over z, x), mp: 16 (over y, core).
Axes of the slice: x: 4, y: 8, z: 8, core: 2. Of those that a mesh axis runs over, the one named last changes fastest.
Arguments:
- grad: bfloat16 [32, 1, 256, 36864], P('dp', None, None, 'mp'), may hold values from -12 to 12
- error: bfloat16 [32, 1, 256, 36864], P('dp', None, None, 'mp'), may hold values from -6 to 6
- q_init: float32 [1, 36864, 32], P(None, 'mp'), may hold values from -0.03125 to 0.03125
Outputs:
- approx: bfloat16 [1, 256, 36864], P(None, None, 'mp')
- q_new: float32 [1, 36864, 32], P(None, 'mp')
All inputs are finite; a program needn't handle non-finite values.
Results may differ from a plain program's by a relative error of at most 0.0083.
Values sent between devices are 32-bit elements; how exact they have to be, the bound alone decides.
No kernel may reach another device: no remote copies, remote signals or barrier semaphores. Data moves between devices by JAX's collectives and lax.ppermute only.
A program may use at most 64 MiB of HBM per device.

v0:
```python
import jax
import jax.numpy as jnp
from jax import lax
from jax.sharding import PartitionSpec as P


def solve_one(low, pmat):
    return jax.scipy.linalg.solve_triangular(low, pmat.T, lower=True).T


def local(grad, error, q_init):
    highest = lax.Precision.HIGHEST
    corrected = (grad[0].astype(jnp.float32) + error[0].astype(jnp.float32)).astype(jnp.bfloat16)
    q_low = q_init.astype(jnp.bfloat16)
    p_part = jnp.einsum("lrf,lfk->lrk", corrected, q_low, preferred_element_type=jnp.float32)
    p_sum = lax.psum(p_part, ("dp", "mp"))
    gram = jnp.einsum("lrk,lrj->lkj", p_sum, p_sum, precision=highest)
    lower = jnp.linalg.cholesky(gram)
    basis = jax.vmap(solve_one)(lower, p_sum)
    basis_low = basis.astype(jnp.bfloat16)
    q_part = jnp.einsum("lrf,lrk->lfk", corrected, basis_low, preferred_element_type=jnp.float32)
    q_new = lax.psum(q_part, "dp")
    approx = jnp.einsum("lrk,lfk->lrf", basis, q_new, precision=highest) / lax.axis_size("dp")
    return (approx.astype(jnp.bfloat16), q_new)


def solution(mesh):
    placed = (P("dp", None, None, "mp"), P("dp", None, None, "mp"), P(None, "mp", None))
    return jax.shard_map(
        local,
        mesh=mesh,
        in_specs=placed,
        out_specs=(P(None, None, "mp"), P(None, "mp", None)),
        check_vma=False,
    )
```

profile of v0, /device:TPU:32, one launch (start us, length us, event | category | flops | bytes accessed | tf_op | source)
XLA Modules:
  0.0 283.5 jit_solution(694716732896514958)
XLA Ops:
  7.2 0.0 copy-start
  7.2 0.0 copy-start.1
  7.2 0.0 all-reduce.2.cloned.1.call-start
  7.2 2.2 convolution_bitcast_fusion.1
  9.5 102.7 %psum.14 = f32[1,256,32]{1,2,0:T(8,128)S(1)} all-reduce(f32[1,256,32]{1,2,0:T(8,128)S(1)} %convolution_bitcast_fusion.1), channel_id=1, replica_groups=mesh['dp'=32,'mp'=16] {'dp','mp'}, use_global_device_ids=true, to_apply=%region_0.0 | all-reduce | flops 8192 | bytes 65536 | tf_op jit(solution)/shard_map/psum | solution.py:16
  112.2 0.2 fusion.10
  112.3 0.1 copy.6
  112.4 2.9 %custom-call.8 = f32[1,32,32]{2,1,0:T(8,128)S(1)} custom-call(f32[1,32,32]{2,1,0:T(8,128)S(1)} %fusion.14), custom_call_target="Cholesky" | custom-call | tf_op jit(solution)/shard_map/jit(cholesky)/cholesky | solution.py:18
  115.4 0.6 compare_reduce_fusion
  116.0 0.7 fusion.12
  116.7 2.4 custom-call.9
  119.1 0.2 fusion.8
  119.4 0.0 copy-done
  119.4 0.0 copy-done.1
  119.4 1.1 convolution_bitcast_fusion
  120.5 0.0 all-reduce.2.cloned.1.call-update
  120.5 151.3 %all-reduce.2.cloned.1.call-done = f32[1,2304,32]{1,2,0:T(8,128)} async-done(((f32[1,2304,32]{1,2,0:T(8,128)}), f32[1,2304,32]{1,2,0:T(8,128)}) %all-reduce.2.cloned.1.call-update) | async-done | bytes 294928 | tf_op jit(solution)/shard_map/psum | solution.py:22
  271.8 0.0 copy-start.2
  271.8 4.1 %fusion.1 = bf16[1,256,2304]{2,1,0:T(8,128)(2,1)} fusion(f32[32,256]{1,0:T(8,128)S(1)} %fusion.8, f32[1,2304,32]{1,2,0:T(8,128)} %all-reduce.2.cloned.1.call-done), kind=kOutput, calls=%fused_computation.2 | convolution fusion | flops 227672064 | bytes 1507328 | tf_op jit(solution)/shard_map/lrk,lfk->lrf/dot_general | solution.py:23
  275.9 0.0 copy-done.2
  275.9 0.7 copy.9
  (2 shorter events, 0.0 us)
Async XLA Ops:
  7.2 112.2 %copy-start = (bf16[1,1,256,2304]{3,2,1,0:T(8,128)(2,1)S(1)}, bf16[1,1,256,2304]{3,2,1,0:T(8,128)(2,1)}, u32[]{:S(2)}) copy-start(bf16[1,1,256,2304]{3,2,1,0:T(8,128)(2,1)} %param.4) | copy-start | bytes 3538948
  7.2 112.2 %copy-start.1 = (bf16[1,1,256,2304]{3,2,1,0:T(8,128)(2,1)S(1)}, bf16[1,1,256,2304]{3,2,1,0:T(8,128)(2,1)}, u32[]{:S(2)}) copy-start(bf16[1,1,256,2304]{3,2,1,0:T(8,128)(2,1)} %param.3) | copy-start | bytes 3538948
  7.2 264.6 %all-reduce.2.cloned.1.call-start = ((), (), s32[]{:S(2)}) async-start(), calls=%async_computation | async-start | bytes 589824 | tf_op jit(solution)/shard_map/psum | solution.py:22
  271.8 4.1 %copy-start.2 = (f32[1,2304,32]{1,2,0:T(8,128)S(1)}, f32[1,2304,32]{1,2,0:T(8,128)}, u32[]{:S(2)}) copy-start(f32[1,2304,32]{1,2,0:T(8,128)} %all-reduce.2.cloned.1.call-done) | copy-start | bytes 884740
Sparse Core Ops, SparseCore 0:
  120.7 151.1 all-reduce.1
where the time goes:
time: 284 us; the launch traced here: 283 us
  waiting for transfers between devices  151 us (53%)
  blocking collectives  103 us (36%)
  between operations  14.1 us (5%)
  matrix products  7.88 us (3%)
  other arithmetic  6.69 us (2%)
    psum x1, waiting for transfers between devices, local(): q_new = lax.psum(q_part, 'dp')  151 us
    psum x1, blocking collectives, local(): p_sum = lax.psum(p_part, ('dp', 'mp'))  103 us
  transfers between devices with their start and end apart: 1, of which 1 were waited for; matrix products, arithmetic and copies ran while one was open for 0% of the time, Pallas kernels for 0%

commit v1 on v0

v1 whole, which is shorter than its diff:
```python
import jax
import jax.numpy as jnp
import numpy as np
from jax import lax
from jax.sharding import PartitionSpec as P

HIGHEST = lax.Precision.HIGHEST
BOTH = ("dp", "mp")
SIDES = {"z": 8, "x": 4, "y": 8, "c": 2}


def groups_along(axes):
    names = list(SIDES)
    ids = np.arange(512).reshape(tuple(SIDES.values()))
    inner = [names.index(a) for a in axes]
    outer = [i for i in range(4) if i not in inner]
    size = int(np.prod([ids.shape[i] for i in inner]))
    return np.transpose(ids, outer + inner).reshape(-1, size).tolist()


def sum_along(x, axes):
    groups = groups_along(axes)
    sent = jnp.broadcast_to(x[None], (len(groups[0]),) + x.shape)
    return jnp.sum(lax.all_to_all(sent, BOTH, 0, 0, axis_index_groups=groups), axis=0)


def pieces(x, count):
    out = []
    for _ in range(count):
        top = lax.reduce_precision(x, 8, 7)
        out.append(top.astype(jnp.bfloat16))
        x = x - top
    return out


def dot(a, b, dims, **kw):
    return lax.dot_general(a, b, (dims, ((), ())), preferred_element_type=jnp.float32, **kw)


def local(grad, error, q_init):
    corrected = (grad[0, 0].astype(jnp.float32) + error[0, 0].astype(jnp.float32)).astype(jnp.bfloat16)
    q_low = q_init[0].astype(jnp.bfloat16)
    p = dot(q_low, corrected, ((0,), (1,)))
    for axes in ("xc", "z", "y"):
        p = sum_along(p, axes)
    stacked = dot(jnp.concatenate(pieces(p, 3), axis=0), corrected, ((1,), (0,)))
    raw = stacked[:32] + stacked[32:64] + stacked[64:]
    mine = jnp.sum(lax.all_to_all(raw, "dp", 0, 0, tiled=True), axis=0)
    raw = lax.all_to_all(jnp.broadcast_to(mine[None], raw.shape), "dp", 0, 0, tiled=True)
    gram = dot(p, p, ((1,), (1,)), precision=HIGHEST)
    lower = jnp.linalg.cholesky(gram)
    inverse = jax.scipy.linalg.solve_triangular(lower, jnp.eye(32, dtype=jnp.float32), lower=True)
    basis = dot(inverse, p, ((1,), (0,)), precision=HIGHEST)
    q_new = dot(inverse, raw, ((1,), (0,)), precision=HIGHEST)
    b1, b2 = pieces(basis, 2)
    q1, q2 = pieces(q_new, 2)
    left = jnp.concatenate([b1, b2, b1], axis=0)
    right = jnp.concatenate([q1, q1, q2], axis=0)
    approx = dot(left, right, ((0,), (0,))) / lax.axis_size("dp")
    return (approx.astype(jnp.bfloat16)[None], q_new.T[None])


def solution(mesh):
    placed = (P("dp", None, None, "mp"), P("dp", None, None, "mp"), P(None, "mp", None))
    return jax.shard_map(
        local,
        mesh=mesh,
        in_specs=placed,
        out_specs=(P(None, None, "mp"), P(None, "mp", None)),
        check_vma=False,
    )
```

time: 284 us -> 90.2 us (0.32)
  the two profiles are of different devices: /device:TPU:32 before, /device:TPU:8 now
where the time goes in v1:
time: 90.2 us; the launch traced here: 89.8 us
  blocking collectives  49.8 us (55%)
  waiting for transfers between devices  16.8 us (19%)
  starting transfers between devices  7.75 us (9%)
  other arithmetic  6.99 us (8%)
  matrix products  5.71 us (6%)
  local copies, waits for them, and re-layouts  2.07 us (2%)
    all_to_all x3, blocking collectives, sum_along(): lax.all_to_all(sent, BOTH, 0, 0, axis_index_groups=groups)  49.8 us
    all_to_all x1, waiting for transfers between devices, local(): lax.all_to_all(jnp.broadcast_to(mine[None], raw.shape), 'dp', 0, 0, tiled...  8.54 us
    all_to_all x1, waiting for transfers between devices, local(): mine = jnp.sum(lax.all_to_all(raw, 'dp', 0, 0, tiled=True), axis=0)  8.24 us
    dot_general x6, matrix products, dot(): lax.dot_general(a, b, (dims, ((), ())), preferred_element_type=jnp.float3...  5.49 us
    all_to_all x1, starting transfers between devices, local(): lax.all_to_all(jnp.broadcast_to(mine[None], raw.shape), 'dp', 0, 0, tiled...  3.87 us
    all_to_all x1, starting transfers between devices, local(): mine = jnp.sum(lax.all_to_all(raw, 'dp', 0, 0, tiled=True), axis=0)  3.87 us
    another operation x3, other arithmetic, local(): lower = jnp.linalg.cholesky(gram)  3.6 us
    another operation x2, other arithmetic, local(): jax.scipy.linalg.solve_triangular(lower, jnp.eye(32, dtype=jnp.float32),...  3.09 us
  transfers between devices with their start and end apart: 2, of which 2 were waited for; matrix products, arithmetic and copies ran while one was open for 8% of the time, Pallas kernels for 0%

profile of v1, /device:TPU:8, one launch (start us, length us, event | category | flops | bytes accessed | tf_op | source)
XLA Modules:
  0.0 89.8 jit_solution(17626295476918508856)
XLA Ops:
  0.6 2.1 %convolution_bitcast_fusion = f32[32,256]{1,0:T(8,128)S(1)} fusion(bf16[1,1,256,2304]{3,2,1,0:T(8,128)(2,1)} %param.4, bf16[1,1,256,2304]{3,2,1,0:T(8,128)(2,1)} %param.3, f32[1,2304,32]{1,2,0:T(8,128)} %param.5), kind=kOutput, calls=%fused_computation.5 | convolution fusion | flops 40181760 | bytes 2686976 | tf_op jit(solution)/shard_map/dot_general | solution.py:37
  2.7 0.1 broadcast_in_dim.13
  2.8 11.6 %all_to_all.33 = f32[8,32,256]{2,1,0:T(8,128)S(1)} all-to-all(f32[8,32,256]{2,1,0:T(8,128)S(1)} %broadcast_in_dim.13), channel_id=1, replica_groups={{0,1,16,17,32,33,48,49},{2,3,18,19,34,35,50,51},{4,5,20,21,36,37,52,53}..., dimensions={0} | all-to-all | bytes 524288 | tf_op jit(solution)/shard_map/all_to_all | solution.py:24
  14.4 0.0 copy-start.1
  14.5 0.0 copy-start
  14.5 21.8 %all_to_all.34 = f32[8,32,256]{2,1,0:T(8,128)S(1)} all-to-all(f32[8,32,256]{2,1,0:T(8,128)S(1)} %broadcast_in_dim.14), channel_id=1, replica_groups={{0,64,128,192,256,320,384,448},{1,65,129,193,257,321,385,449},{2,66,130..., dimensions={0} | all-to-all | bytes 524288 | tf_op jit(solution)/shard_map/all_to_all | solution.py:24
  36.3 16.4 %all_to_all.35 = f32[8,32,256]{2,1,0:T(8,128)S(1)} all-to-all(f32[8,32,256]{2,1,0:T(8,128)S(1)} %broadcast_in_dim.15), channel_id=1, replica_groups={{0,2,4,6,8,10,12,14},{1,3,5,7,9,11,13,15},{16,18,20,22,24,26,28,30},{17..., dimensions={0} | all-to-all | bytes 524288 | tf_op jit(solution)/shard_map/all_to_all | solution.py:24
  52.7 0.0 copy-done.1
  52.7 0.0 copy-done
  52.7 0.5 fusion.3
  53.2 1.0 %copy.9 = f32[32,1,2304]{2,1,0:T(1,128)} copy(f32[32,1,2304]{2,0,1:T(8,128)S(1)} %fusion.13) | data formatting | bytes 589824 | tf_op jit(solution)/shard_map/all_to_all | solution.py:48
  54.3 3.9 %all-to-all-start.3 = ((f32[32,1,2304]{2,1,0:T(1,128)}), f32[32,1,2304]{2,1,0:T(1,128)S(1)}, u32[]{:S(2)}, u32[]{:S(2)}) async-start(f32[32,1,2304]{2,1,0:T(1,128)} %copy.9), calls=%async_computation.3 | async-start | bytes 589824 | tf_op jit(solution)/shard_map/all_to_all | solution.py:48
  58.1 0.2 fusion.39
  58.3 0.1 copy.8
  58.4 2.9 %cholesky.17 = f32[32,32]{1,0:T(8,128)S(1)} custom-call(f32[32,32]{1,0:T(8,128)S(1)} %fusion.36), custom_call_target="Cholesky" | custom-call | tf_op jit(solution)/shard_map/jit(cholesky)/cholesky | solution.py:51
  61.3 0.6 compare_reduce_fusion
  62.0 8.2 %all-to-all-done.3 = f32[32,1,2304]{2,1,0:T(1,128)S(1)} async-done(((f32[32,1,2304]{2,1,0:T(1,128)}), f32[32,1,2304]{2,1,0:T(1,128)S(1)}, u32[]{:S(2)}, u32[]{:S(2)}) %all-to-all-start.3) | async-done | bytes 294944 | tf_op jit(solution)/shard_map/all_to_all | solution.py:48
  70.2 0.2 reduce_sum.39
  70.4 0.9 broadcast_in_dim.16
  71.3 3.9 %all-to-all-start.4 = ((f32[32,1,2304]{2,1,0:T(1,128)}), f32[32,1,2304]{2,1,0:T(1,128)S(1)}, u32[]{:S(2)}, u32[]{:S(2)}) async-start(f32[32,1,2304]{2,1,0:T(1,128)} %broadcast_in_dim.16), calls=%async_computation.4 | async-start | bytes 589824 | tf_op jit(solution)/shard_map/all_to_all | solution.py:49
  75.2 0.7 fusion.33
  75.8 2.4 %custom-call.7 = f32[1,32,32]{1,2,0:T(8,128)S(1)} custom-call(f32[1,32,32]{2,1,0:T(8,128)S(1)} %fusion.33), custom_call_target="InvertDiagBlocksLowerTriangular" | custom-call | tf_op jit(solution)/shard_map/jit(_solve_triangular)/triangular_solve | solution.py:52
  78.3 0.2 fusion.34
  78.5 0.2 fusion.30
  78.7 8.5 %all-to-all-done.4 = f32[32,1,2304]{2,1,0:T(1,128)S(1)} async-done(((f32[32,1,2304]{2,1,0:T(1,128)}), f32[32,1,2304]{2,1,0:T(1,128)S(1)}, u32[]{:S(2)}, u32[]{:S(2)}) %all-to-all-start.4) | async-done | bytes 294944 | tf_op jit(solution)/shard_map/all_to_all | solution.py:49
  87.2 1.1 %reduce-precision_convert_fusion = (bf16[32,2304]{1,0:T(8,128)(2,1)S(1)}, bf16[32,2304]{1,0:T(8,128)(2,1)S(1)}, f32[32,2304]{1,0:T(8,128)}) fusion(f32[32,32]{1,0:T(8,128)S(1)} %fusion.34, f32[32,1,2304]{2,1,0:T(1,128)S(1)} %all-to-all-done.4), kind=kOutput, calls=%fused_computation.13 | convolution fusion | flops 28680192 | bytes 888832 | tf_op jit(solution)/shard_map/dot_general | solution.py:37
  88.3 1.5 %fusion.1 = bf16[1,256,2304]{2,1,0:T(8,128)(2,1)} fusion(bf16[32,2304]{1,0:T(8,128)(2,1)S(1)} %get-tuple-element.3, bf16[32,2304]{1,0:T(8,128)(2,1)S(1)} %get-tuple-element.2, bf16[32,256]{1,0:T(8,128)(2,1)S(1)} %get-tuple-element.5, bf16[32,256]{1,0:T(8,128)(2,1)S(1)} %get-tuple-element.4), kind=kOutput, calls=%fused_computation.2 | convolution fusion | flops 115900416 | bytes 1507328 | tf_op jit(solution)/shard_map/dot_general | solution.py:37
  (9 shorter events, 0.2 us)
Async XLA Ops:
  14.4 38.3 %copy-start.1 = (bf16[1,1,256,2304]{3,2,1,0:T(8,128)(2,1)S(1)}, bf16[1,1,256,2304]{3,2,1,0:T(8,128)(2,1)}, u32[]{:S(2)}) copy-start(bf16[1,1,256,2304]{3,2,1,0:T(8,128)(2,1)} %param.3) | copy-start | bytes 3538948
  14.5 38.3 %copy-start = (bf16[1,1,256,2304]{3,2,1,0:T(8,128)(2,1)S(1)}, bf16[1,1,256,2304]{3,2,1,0:T(8,128)(2,1)}, u32[]{:S(2)}) copy-start(bf16[1,1,256,2304]{3,2,1,0:T(8,128)(2,1)} %param.4) | copy-start | bytes 3538948
  54.3 16.0 %all-to-all-start.3 = ((f32[32,1,2304]{2,1,0:T(1,128)}), f32[32,1,2304]{2,1,0:T(1,128)S(1)}, u32[]{:S(2)}, u32[]{:S(2)}) async-start(f32[32,1,2304]{2,1,0:T(1,128)} %copy.9), calls=%async_computation.3 | async-start | bytes 589824 | tf_op jit(solution)/shard_map/all_to_all | solution.py:48
  71.3 15.9 %all-to-all-start.4 = ((f32[32,1,2304]{2,1,0:T(1,128)}), f32[32,1,2304]{2,1,0:T(1,128)S(1)}, u32[]{:S(2)}, u32[]{:S(2)}) async-start(f32[32,1,2304]{2,1,0:T(1,128)} %broadcast_in_dim.16), calls=%async_computation.4 | async-start | bytes 589824 | tf_op jit(solution)/shard_map/all_to_all | solution.py:49

commit v2 on v1

--- a/solution.py
+++ b/solution.py
@@ -6,22 +6,30 @@
 
 HIGHEST = lax.Precision.HIGHEST
 BOTH = ("dp", "mp")
-SIDES = {"z": 8, "x": 4, "y": 8, "c": 2}
+BITS = ("z2", "z1", "z0", "x1", "x0", "y2", "y1", "y0", "c")
+NEAR = ("x1", "x0", "y0", "c")
+FAR = ("z2", "z1", "z0", "y2", "y1")
 
 
-def groups_along(axes):
-    names = list(SIDES)
-    ids = np.arange(512).reshape(tuple(SIDES.values()))
-    inner = [names.index(a) for a in axes]
-    outer = [i for i in range(4) if i not in inner]
-    size = int(np.prod([ids.shape[i] for i in inner]))
-    return np.transpose(ids, outer + inner).reshape(-1, size).tolist()
+def groups_along(bits):
+    ids = np.arange(512).reshape((2,) * 9)
+    inner = [i for i, b in enumerate(BITS) if b in bits]
+    outer = [i for i, b in enumerate(BITS) if b not in bits]
+    return np.transpose(ids, outer + inner).reshape(-1, 2 ** len(inner)).tolist()
 
 
-def sum_along(x, axes):
-    groups = groups_along(axes)
-    sent = jnp.broadcast_to(x[None], (len(groups[0]),) + x.shape)
-    return jnp.sum(lax.all_to_all(sent, BOTH, 0, 0, axis_index_groups=groups), axis=0)
+def exchange(x, bits):
+    return lax.all_to_all(x, BOTH, 0, 0, axis_index_groups=groups_along(bits))
+
+
+def spread(x, count):
+    return jnp.broadcast_to(x[None], (count,) + x.shape)
+
+
+def sum_all(p):
+    part = jnp.sum(exchange(p.reshape(16, p.shape[0] // 16, p.shape[1]), NEAR), axis=0)
+    part = jnp.sum(exchange(spread(part, 32), FAR), axis=0)
+    return exchange(spread(part, 16), NEAR).reshape(p.shape)
 
 
 def pieces(x, count):
@@ -41,8 +49,7 @@
     corrected = (grad[0, 0].astype(jnp.float32) + error[0, 0].astype(jnp.float32)).astype(jnp.bfloat16)
     q_low = q_init[0].astype(jnp.bfloat16)
     p = dot(q_low, corrected, ((0,), (1,)))
-    for axes in ("xc", "z", "y"):
-        p = sum_along(p, axes)
+    p = sum_all(p)
     stacked = dot(jnp.concatenate(pieces(p, 3), axis=0), corrected, ((1,), (0,)))
     raw = stacked[:32] + stacked[32:64] + stacked[64:]
     mine = jnp.sum(lax.all_to_all(raw, "dp", 0, 0, tiled=True), axis=0)

time: 90.2 us -> 89.7 us (level)
  blocking collectives: 49.8 us -> 46.1 us
  waiting for transfers between devices: 16.8 us -> 19.7 us
    all_to_all x3, blocking collectives: 49.8 us -> 46.1 us  [exchange(): return lax.all_to_all(x, BOTH, 0, 0, axis_index_groups=groups_along(bits))]
    all_to_all x1, waiting for transfers between devices: 8.24 us -> 10.3 us  [local(): mine = jnp.sum(lax.all_to_all(raw, 'dp', 0, 0, tiled=True), axis=0)]
where the time goes in v2:
time: 89.7 us; the launch traced here: 89.3 us
  blocking collectives  46.1 us (51%)
  waiting for transfers between devices  19.7 us (22%)
  starting transfers between devices  7.76 us (9%)
  other arithmetic  7 us (8%)
  matrix products  5.87 us (7%)
  local copies, waits for them, and re-layouts  2.09 us (2%)
    all_to_all x3, blocking collectives, exchange(): return lax.all_to_all(x, BOTH, 0, 0, axis_index_groups=groups_along(bits))  46.1 us
    all_to_all x1, waiting for transfers between devices, local(): mine = jnp.sum(lax.all_to_all(raw, 'dp', 0, 0, tiled=True), axis=0)  10.3 us
    all_to_all x1, waiting for transfers between devices, local(): lax.all_to_all(jnp.broadcast_to(mine[None], raw.shape), 'dp', 0, 0, tiled...  9.39 us
    dot_general x6, matrix products, dot(): lax.dot_general(a, b, (dims, ((), ())), preferred_element_type=jnp.float3...  5.65 us
    all_to_all x1, starting transfers between devices, local(): lax.all_to_all(jnp.broadcast_to(mine[None], raw.shape), 'dp', 0, 0, tiled...  3.89 us
    all_to_all x1, starting transfers between devices, local(): mine = jnp.sum(lax.all_to_all(raw, 'dp', 0, 0, tiled=True), axis=0)  3.87 us
    another operation x3, other arithmetic, local(): lower = jnp.linalg.cholesky(gram)  3.6 us
    another operation x2, other arithmetic, local(): jax.scipy.linalg.solve_triangular(lower, jnp.eye(32, dtype=jnp.float32),...  3.09 us
  transfers between devices with their start and end apart: 2, of which 2 were waited for; matrix products, arithmetic and copies ran while one was open for 8% of the time, Pallas kernels for 0%

profile of v2, /device:TPU:8, one launch (start us, length us, event | category | flops | bytes accessed | tf_op | source)
XLA Modules:
  0.0 89.3 jit_solution(15561981101806404140)
XLA Ops:
  0.6 0.0 copy-start
  0.6 0.0 copy-start.1
  0.7 2.2 %convolution_bitcast_fusion = f32[32,256]{1,0:T(8,128)S(1)} fusion(bf16[1,1,256,2304]{3,2,1,0:T(8,128)(2,1)} %param.4, bf16[1,1,256,2304]{3,2,1,0:T(8,128)(2,1)} %param.3, f32[1,2304,32]{1,2,0:T(8,128)} %param.5), kind=kOutput, calls=%fused_computation.5 | convolution fusion | flops 40181760 | bytes 2686976 | tf_op jit(solution)/shard_map/dot_general | solution.py:45
  2.9 0.1 reshape.36
  3.0 13.1 %all_to_all.33 = f32[16,2,256]{2,1,0:T(2,128)S(1)} all-to-all(f32[16,2,256]{2,1,0:T(2,128)S(1)} %reshape.36), channel_id=1, replica_groups={{0,1,2,3,16,17,18,19,32,33,34,35,48,49,50,51},{4,5,6,7,20,21,22,23,36,3..., dimensions={0} | all-to-all | bytes 65536 | tf_op jit(solution)/shard_map/all_to_all | solution.py:22
  16.1 24.4 %all_to_all.34 = f32[32,2,256]{2,1,0:T(2,128)S(1)} all-to-all(f32[32,2,256]{2,1,0:T(2,128)S(1)} %broadcast_in_dim.11), channel_id=1, replica_groups={{0,4,8,12,64,68,72,76,128,132,136,140,192,196,200,204,256,260,264,268,3..., dimensions={0} | all-to-all | bytes 131072 | tf_op jit(solution)/shard_map/all_to_all | solution.py:22
  40.6 8.6 %all_to_all.35 = f32[16,2,256]{2,1,0:T(2,128)S(1)} all-to-all(f32[16,2,256]{2,1,0:T(2,128)S(1)} %broadcast_in_dim.12), channel_id=1, replica_groups={{0,1,2,3,16,17,18,19,32,33,34,35,48,49,50,51},{4,5,6,7,20,21,22,23,36,3..., dimensions={0} | all-to-all | bytes 65536 | tf_op jit(solution)/shard_map/all_to_all | solution.py:22
  49.3 0.0 copy-done
  49.3 0.0 copy-done.1
  49.3 0.5 fusion.3
  49.8 1.0 %copy.12 = f32[32,1,2304]{2,1,0:T(1,128)} copy(f32[32,1,2304]{2,0,1:T(8,128)S(1)} %fusion.13) | data formatting | bytes 589824 | tf_op jit(solution)/shard_map/all_to_all | solution.py:55
  50.8 3.9 %all-to-all-start.3 = ((f32[32,1,2304]{2,1,0:T(1,128)}), f32[32,1,2304]{2,1,0:T(1,128)S(1)}, u32[]{:S(2)}, u32[]{:S(2)}) async-start(f32[32,1,2304]{2,1,0:T(1,128)} %copy.12), calls=%async_computation.3 | async-start | bytes 589824 | tf_op jit(solution)/shard_map/all_to_all | solution.py:55
  54.7 0.2 fusion.39
  54.8 0.1 copy.11
  54.9 2.9 %cholesky.17 = f32[32,32]{1,0:T(8,128)S(1)} custom-call(f32[32,32]{1,0:T(8,128)S(1)} %fusion.36), custom_call_target="Cholesky" | custom-call | tf_op jit(solution)/shard_map/jit(cholesky)/cholesky | solution.py:58
  57.9 0.6 compare_reduce_fusion
  58.5 10.3 %all-to-all-done.3 = f32[32,1,2304]{2,1,0:T(1,128)S(1)} async-done(((f32[32,1,2304]{2,1,0:T(1,128)}), f32[32,1,2304]{2,1,0:T(1,128)S(1)}, u32[]{:S(2)}, u32[]{:S(2)}) %all-to-all-start.3) | async-done | bytes 294944 | tf_op jit(solution)/shard_map/all_to_all | solution.py:55
  68.8 0.2 reduce_sum.29
  69.0 0.9 broadcast_in_dim.14
  69.8 3.9 %all-to-all-start.4 = ((f32[32,1,2304]{2,1,0:T(1,128)}), f32[32,1,2304]{2,1,0:T(1,128)S(1)}, u32[]{:S(2)}, u32[]{:S(2)}) async-start(f32[32,1,2304]{2,1,0:T(1,128)} %broadcast_in_dim.14), calls=%async_computation.4 | async-start | bytes 589824 | tf_op jit(solution)/shard_map/all_to_all | solution.py:56
  73.7 0.7 fusion.33
  74.4 2.4 %custom-call.7 = f32[1,32,32]{1,2,0:T(8,128)S(1)} custom-call(f32[1,32,32]{2,1,0:T(8,128)S(1)} %fusion.33), custom_call_target="InvertDiagBlocksLowerTriangular" | custom-call | tf_op jit(solution)/shard_map/jit(_solve_triangular)/triangular_solve | solution.py:59
  76.8 0.2 fusion.34
  77.1 0.2 fusion.30
  77.2 9.4 %all-to-all-done.4 = f32[32,1,2304]{2,1,0:T(1,128)S(1)} async-done(((f32[32,1,2304]{2,1,0:T(1,128)}), f32[32,1,2304]{2,1,0:T(1,128)S(1)}, u32[]{:S(2)}, u32[]{:S(2)}) %all-to-all-start.4) | async-done | bytes 294944 | tf_op jit(solution)/shard_map/all_to_all | solution.py:56
  86.6 1.1 %reduce-precision_convert_fusion = (bf16[32,2304]{1,0:T(8,128)(2,1)S(1)}, bf16[32,2304]{1,0:T(8,128)(2,1)S(1)}, f32[32,2304]{1,0:T(8,128)}) fusion(f32[32,32]{1,0:T(8,128)S(1)} %fusion.34, f32[32,1,2304]{2,1,0:T(1,128)S(1)} %all-to-all-done.4), kind=kOutput, calls=%fused_computation.13 | convolution fusion | flops 28680192 | bytes 888832 | tf_op jit(solution)/shard_map/dot_general | solution.py:45
  87.7 1.5 %fusion.1 = bf16[1,256,2304]{2,1,0:T(8,128)(2,1)} fusion(bf16[32,2304]{1,0:T(8,128)(2,1)S(1)} %get-tuple-element.3, bf16[32,2304]{1,0:T(8,128)(2,1)S(1)} %get-tuple-element.2, bf16[32,256]{1,0:T(8,128)(2,1)S(1)} %get-tuple-element.5, bf16[32,256]{1,0:T(8,128)(2,1)S(1)} %get-tuple-element.4), kind=kOutput, calls=%fused_computation.2 | convolution fusion | flops 115900416 | bytes 1507328 | tf_op jit(solution)/shard_map/dot_general | solution.py:45
  (9 shorter events, 0.2 us)
Async XLA Ops:
  0.6 48.6 %copy-start = (bf16[1,1,256,2304]{3,2,1,0:T(8,128)(2,1)S(1)}, bf16[1,1,256,2304]{3,2,1,0:T(8,128)(2,1)}, u32[]{:S(2)}) copy-start(bf16[1,1,256,2304]{3,2,1,0:T(8,128)(2,1)} %param.4) | copy-start | bytes 3538948
  0.6 48.6 %copy-start.1 = (bf16[1,1,256,2304]{3,2,1,0:T(8,128)(2,1)S(1)}, bf16[1,1,256,2304]{3,2,1,0:T(8,128)(2,1)}, u32[]{:S(2)}) copy-start(bf16[1,1,256,2304]{3,2,1,0:T(8,128)(2,1)} %param.3) | copy-start | bytes 3538948
  50.8 18.0 %all-to-all-start.3 = ((f32[32,1,2304]{2,1,0:T(1,128)}), f32[32,1,2304]{2,1,0:T(1,128)S(1)}, u32[]{:S(2)}, u32[]{:S(2)}) async-start(f32[32,1,2304]{2,1,0:T(1,128)} %copy.12), calls=%async_computation.3 | async-start | bytes 589824 | tf_op jit(solution)/shard_map/all_to_all | solution.py:55
  69.8 16.8 %all-to-all-start.4 = ((f32[32,1,2304]{2,1,0:T(1,128)}), f32[32,1,2304]{2,1,0:T(1,128)S(1)}, u32[]{:S(2)}, u32[]{:S(2)}) async-start(f32[32,1,2304]{2,1,0:T(1,128)} %broadcast_in_dim.14), calls=%async_computation.4 | async-start | bytes 589824 | tf_op jit(solution)/shard_map/all_to_all | solution.py:56

commit v3 on v2

v3 whole, which is shorter than its diff:
```python
import jax
import jax.numpy as jnp
import numpy as np
from jax import lax
from jax.experimental import pallas as pl
from jax.experimental.pallas import tpu as pltpu
from jax.sharding import PartitionSpec as P

HIGHEST = lax.Precision.HIGHEST
BOTH = ("dp", "mp")
BITS = ("z2", "z1", "z0", "x1", "x0", "y2", "y1", "y0", "c")
NEAR = ("x1", "x0", "y0", "c")
FAR = ("z2", "z1", "z0", "y2", "y1")
ROWS, RANK, COLS, PEERS = 256, 32, 2304, 32
LANES = 128
TILES = COLS // LANES
WIDE = 768
LIMIT = 12 * 1024 * 1024
F32, BF16 = jnp.float32, jnp.bfloat16


def groups_along(bits):
    ids = np.arange(512).reshape((2,) * 9)
    inner = [i for i, b in enumerate(BITS) if b in bits]
    outer = [i for i, b in enumerate(BITS) if b not in bits]
    return np.transpose(ids, outer + inner).reshape(-1, 2 ** len(inner)).tolist()


def exchange(x, bits):
    return lax.all_to_all(x, BOTH, 0, 0, axis_index_groups=groups_along(bits))


def spread(x, count):
    return jnp.broadcast_to(x[None], (count,) + x.shape)


def sum_all(p):
    part = jnp.sum(exchange(p.reshape(16, p.shape[0] // 16, p.shape[1]), NEAR), axis=0)
    part = jnp.sum(exchange(spread(part, 32), FAR), axis=0)
    return exchange(spread(part, 16), NEAR).reshape(p.shape)


def cut(x, count):
    out = []
    for _ in range(count):
        top = x.astype(BF16)
        out.append(top)
        x = x - top.astype(F32)
    return out


def pieces(x, count):
    out = []
    for _ in range(count):
        top = lax.reduce_precision(x, 8, 7)
        out.append(top.astype(BF16))
        x = x - top
    return out


def dot(a, b, dims, **kw):
    return lax.dot_general(a, b, (dims, ((), ())), preferred_element_type=F32, **kw)


def project(grad, error, q_init, p_out, corrected, g, e, q, sems):
    def copies(i):
        cols = pl.ds(i * WIDE, WIDE)
        return [
            pltpu.make_async_copy(src.at[:, cols], dst.at[:, cols], sems.at[i, j])
            for j, (src, dst) in enumerate(((grad, g), (error, e), (q_init, q)))
        ]

    for i in range(COLS // WIDE):
        for copy in copies(i):
            copy.start()
    total = jnp.zeros((RANK, ROWS), F32)
    for i in range(COLS // WIDE):
        for copy in copies(i):
            copy.wait()
        cols = pl.ds(i * WIDE, WIDE)
        both = (g[:, cols].astype(F32) + e[:, cols].astype(F32)).astype(BF16)
        corrected[:, cols] = both
        total = total + dot(q[:, cols].astype(BF16), both, ((1,), (1,)))
    p_out[...] = total


def partial(p, corrected, out):
    left = jnp.concatenate(cut(p[...], 3), axis=0)
    for t in range(0, TILES, 2):
        acc = dot(left, corrected[:, pl.ds(t * LANES, 2 * LANES)], ((1,), (0,)))
        acc = acc[:RANK] + acc[RANK : 2 * RANK] + acc[2 * RANK :]
        for h in range(2):
            for k in range(0, RANK, 8):
                out[pl.ds(k * TILES + t + h, 8, stride=TILES), :] = acc[k : k + 8, h * LANES : (h + 1) * LANES]


def gathered(x, out):
    for t in range(TILES):
        at = [pl.ds(k * TILES + t, 8, stride=TILES) for k in range(0, PEERS, 8)]
        acc = (x[at[0], :] + x[at[1], :]) + (x[at[2], :] + x[at[3], :])
        acc = jnp.broadcast_to(jnp.sum(acc, axis=0, keepdims=True), (8, LANES))
        for rows in at:
            out[rows, :] = acc


def finish(raw, inverse, basis, approx_out, q_out, approx, q_new, sems):
    pending = []
    for i in range(COLS // WIDE):
        parts = []
        for t in range(i * WIDE // LANES, (i + 1) * WIDE // LANES):
            rows = [raw[pl.ds(k * TILES + t, 8, stride=TILES), :] for k in range(0, RANK, 8)]
            parts.append(jnp.concatenate(rows, axis=0))
        r1, r2, r3 = cut(jnp.concatenate(parts, axis=1), 3)
        q = dot(inverse[...], jnp.concatenate([r1, r2, r1, r2, r3, r1], axis=0), ((1,), (0,)))
        cols = pl.ds(i * WIDE, WIDE)
        q_new[:, cols] = q
        q1, q2 = cut(q, 2)
        approx[:, cols] = dot(basis[...], jnp.concatenate([q1, q1, q2], axis=0), ((1,), (0,))).astype(BF16)
        for j, (src, dst) in enumerate(((approx, approx_out), (q_new, q_out))):
            copy = pltpu.make_async_copy(src.at[:, cols], dst.at[:, cols], sems.at[i, j])
            copy.start()
            pending.append(copy)
    for copy in pending:
        copy.wait()


def in_vmem(x):
    return pltpu.with_memory_space_constraint(x, pltpu.VMEM)


def in_hbm(x):
    return pltpu.with_memory_space_constraint(x, pltpu.HBM)


PARAMS = pltpu.CompilerParams(vmem_limit_bytes=LIMIT)
VMEM, HBM = pl.BlockSpec(memory_space=pltpu.VMEM), pl.BlockSpec(memory_space=pltpu.HBM)
CHUNKS = COLS // WIDE
LINEAR = (RANK * TILES, LANES)


def local(grad, error, q_init):
    p, corrected = pl.pallas_call(
        project,
        out_shape=(pltpu.VMEM((RANK, ROWS), F32), pltpu.VMEM((ROWS, COLS), BF16)),
        in_specs=[HBM] * 3,
        out_specs=(VMEM, VMEM),
        scratch_shapes=[
            pltpu.VMEM((ROWS, COLS), BF16),
            pltpu.VMEM((ROWS, COLS), BF16),
            pltpu.VMEM((RANK, COLS), F32),
            pltpu.SemaphoreType.DMA((CHUNKS, 3)),
        ],
        compiler_params=PARAMS,
        name="project",
    )(in_hbm(grad[0, 0]), in_hbm(error[0, 0]), in_hbm(q_init[0].T))
    p = sum_all(p)
    raw = pl.pallas_call(
        partial,
        out_shape=pltpu.VMEM(LINEAR, F32),
        in_specs=[VMEM] * 2,
        out_specs=VMEM,
        compiler_params=PARAMS,
        name="partial",
    )(in_vmem(p), in_vmem(corrected))
    raw = lax.all_to_all(raw.reshape(PEERS, 1, COLS), "dp", 0, 0, tiled=True)
    raw = pl.pallas_call(
        gathered,
        out_shape=pltpu.VMEM(LINEAR, F32),
        in_specs=[VMEM],
        out_specs=VMEM,
        compiler_params=PARAMS,
        name="gathered",
    )(in_vmem(raw.reshape(LINEAR)))
    raw = lax.all_to_all(raw.reshape(PEERS, 1, COLS), "dp", 0, 0, tiled=True).reshape(LINEAR)
    gram = dot(p, p, ((1,), (1,)), precision=HIGHEST)
    lower = jnp.linalg.cholesky(gram)
    inverse = jax.scipy.linalg.solve_triangular(lower, jnp.eye(RANK, dtype=F32), lower=True)
    basis = dot(p, inverse, ((0,), (1,)), precision=HIGHEST) / lax.axis_size("dp")
    b1, b2 = pieces(basis, 2)
    i1, i2, i3 = pieces(inverse, 3)
    approx, q_new = pl.pallas_call(
        finish,
        out_shape=(jax.ShapeDtypeStruct((ROWS, COLS), BF16), jax.ShapeDtypeStruct((RANK, COLS), F32)),
        in_specs=[VMEM] * 3,
        out_specs=(HBM, HBM),
        scratch_shapes=[
            pltpu.VMEM((ROWS, COLS), BF16),
            pltpu.VMEM((RANK, COLS), F32),
            pltpu.SemaphoreType.DMA((CHUNKS, 2)),
        ],
        compiler_params=PARAMS,
        name="finish",
    )(
        in_vmem(raw),
        in_vmem(jnp.concatenate([i1, i1, i2, i2, i1, i3], axis=1)),
        in_vmem(jnp.concatenate([b1, b2, b1], axis=1)),
    )
    return (approx[None], q_new.T[None])


def solution(mesh):
    placed = (P("dp", None, None, "mp"), P("dp", None, None, "mp"), P(None, "mp", None))
    return jax.shard_map(
        local,
        mesh=mesh,
        in_specs=placed,
        out_specs=(P(None, None, "mp"), P(None, "mp", None)),
        check_vma=False,
    )
```

time: 89.7 us -> 87.9 us (0.980)
  Pallas kernels: 0 us -> 5.75 us
  matrix products: 5.87 us -> 0.78 us
  local copies, waits for them, and re-layouts: 2.09 us -> 0.24 us
    pallas_call x0 -> x4, Pallas kernels: none -> 5.75 us  [the longest x1 2.22 us: local(): pl.pallas_call(project, out_shape=(pltpu.VMEM((RANK, ROWS), F32), pltpu.V...]
    dot_general x6 -> x2, matrix products: 5.65 us -> 0.55 us  [dot(): lax.dot_general(a, b, (dims, ((), ())), preferred_element_type=F32, **kw)]
    all_to_all x1 -> x0, local copies, waits for them, and re-layouts: 1.02 us -> none  [local(): mine = jnp.sum(lax.all_to_all(raw, 'dp', 0, 0, tiled=True), axis=0)]
  transfers between devices with their start and end apart: 2 -> 2, of which waited for: 2 -> 2; matrix products, arithmetic and copies ran while one was open for 8% -> 9% of each run, Pallas kernels for 0% -> 0%
where the time goes in v3:
time: 87.9 us; the launch traced here: 87.5 us
  blocking collectives  46.1 us (52%)
  waiting for transfers between devices  19.2 us (22%)
  starting transfers between devices  7.76 us (9%)
  other arithmetic  6.87 us (8%)
  Pallas kernels  5.75 us (7%)
    all_to_all x3, blocking collectives, exchange(): return lax.all_to_all(x, BOTH, 0, 0, axis_index_groups=groups_along(bits))  46.1 us
    all_to_all x1, waiting for transfers between devices, local(): raw = lax.all_to_all(raw.reshape(PEERS, 1, COLS), 'dp', 0, 0, tiled=True)  10.3 us
    all_to_all x1, waiting for transfers between devices, local(): lax.all_to_all(raw.reshape(PEERS, 1, COLS), 'dp', 0, 0, tiled=True)  8.94 us
    all_to_all x1, starting transfers between devices, local(): lax.all_to_all(raw.reshape(PEERS, 1, COLS), 'dp', 0, 0, tiled=True)  3.89 us
    all_to_all x1, starting transfers between devices, local(): raw = lax.all_to_all(raw.reshape(PEERS, 1, COLS), 'dp', 0, 0, tiled=True)  3.87 us
    another operation x3, other arithmetic, local(): lower = jnp.linalg.cholesky(gram)  3.6 us
    another operation x2, other arithmetic, local(): jax.scipy.linalg.solve_triangular(lower, jnp.eye(RANK, dtype=F32), lower=...  3.09 us
    pallas_call x1, Pallas kernels, local(): pl.pallas_call(project, out_shape=(pltpu.VMEM((RANK, ROWS), F32), pltpu.V...  2.22 us
  transfers between devices with their start and end apart: 2, of which 2 were waited for; matrix products, arithmetic and copies ran while one was open for 9% of the time, Pallas kernels for 0%

profile of v3, /device:TPU:8, one launch (start us, length us, event | category | flops | bytes accessed | tf_op | source)
XLA Modules:
  0.0 87.5 jit_solution(2030797703454560332)
XLA Ops:
  0.6 2.2 %project.1 = (f32[32,256]{1,0:T(8,128)S(1)}, bf16[256,2304]{1,0:T(8,128)(2,1)S(1)}) custom-call(bf16[256,2304]{1,0:T(8,128)(2,1)} %bitcast.30, bf16[256,2304]{1,0:T(8,128)(2,1)} %bitcast.31, f32[32,2304]{1,0:T(8,128)} %bitcast.32), custom_call_target="tpu_custom_call" | custom-call | tf_op jit(solution)/shard_map/project/pallas_call | solution.py:142
  2.9 13.1 %all_to_all.25 = f32[16,2,256]{2,1,0:T(2,128)S(1)} all-to-all(f32[16,2,256]{2,1,0:T(2,128)S(1)} %reshape.34), channel_id=1, replica_groups={{0,1,2,3,16,17,18,19,32,33,34,35,48,49,50,51},{4,5,6,7,20,21,22,23,36,3..., dimensions={0} | all-to-all | bytes 65536 | tf_op jit(solution)/shard_map/all_to_all | solution.py:30
  16.0 24.4 %all_to_all.26 = f32[32,2,256]{2,1,0:T(2,128)S(1)} all-to-all(f32[32,2,256]{2,1,0:T(2,128)S(1)} %broadcast_in_dim.10), channel_id=1, replica_groups={{0,4,8,12,64,68,72,76,128,132,136,140,192,196,200,204,256,260,264,268,3..., dimensions={0} | all-to-all | bytes 131072 | tf_op jit(solution)/shard_map/all_to_all | solution.py:30
  40.5 8.6 %all_to_all.27 = f32[16,2,256]{2,1,0:T(2,128)S(1)} all-to-all(f32[16,2,256]{2,1,0:T(2,128)S(1)} %broadcast_in_dim.11), channel_id=1, replica_groups={{0,1,2,3,16,17,18,19,32,33,34,35,48,49,50,51},{4,5,6,7,20,21,22,23,36,3..., dimensions={0} | all-to-all | bytes 65536 | tf_op jit(solution)/shard_map/all_to_all | solution.py:30
  49.1 1.0 %partial.1 = f32[576,128]{1,0:T(8,128)} custom-call(f32[32,256]{1,0:T(8,128)S(1)} %reshape.35.p, bf16[256,2304]{1,0:T(8,128)(2,1)S(1)} %get-tuple-element.7.corrected), custom_call_target="tpu_custom_call" | custom-call | tf_op jit(solution)/shard_map/partial/pallas_call | solution.py:157
  50.2 3.9 %all-to-all-start.3 = ((f32[32,1,2304]{2,1,0:T(1,128)}), f32[32,1,2304]{2,1,0:T(1,128)S(1)}, u32[]{:S(2)}, u32[]{:S(2)}) async-start(f32[32,1,2304]{2,1,0:T(1,128)} %bitcast.4), calls=%async_computation.3 | async-start | bytes 589824 | tf_op jit(solution)/shard_map/all_to_all | solution.py:165
  54.1 0.2 fusion.8
  54.2 0.1 copy.23
  54.3 2.9 %cholesky.17 = f32[32,32]{1,0:T(8,128)S(1)} custom-call(f32[32,32]{1,0:T(8,128)S(1)} %fusion.7), custom_call_target="Cholesky" | custom-call | tf_op jit(solution)/shard_map/jit(cholesky)/cholesky | solution.py:176
  57.3 0.6 compare_reduce_fusion
  57.9 10.3 %all-to-all-done.3 = f32[32,1,2304]{2,1,0:T(1,128)S(1)} async-done(((f32[32,1,2304]{2,1,0:T(1,128)}), f32[32,1,2304]{2,1,0:T(1,128)S(1)}, u32[]{:S(2)}, u32[]{:S(2)}) %all-to-all-start.3) | async-done | bytes 294944 | tf_op jit(solution)/shard_map/all_to_all | solution.py:165
  68.2 0.7 gathered.1
  69.0 3.9 %all-to-all-start.4 = ((f32[32,1,2304]{2,1,0:T(1,128)}), f32[32,1,2304]{2,1,0:T(1,128)S(1)}, u32[]{:S(2)}, u32[]{:S(2)}) async-start(f32[32,1,2304]{2,1,0:T(1,128)} %bitcast.6), calls=%async_computation.4 | async-start | bytes 589824 | tf_op jit(solution)/shard_map/all_to_all | solution.py:174
  72.9 0.7 fusion.2
  73.5 2.4 %custom-call.7 = f32[1,32,32]{1,2,0:T(8,128)S(1)} custom-call(f32[1,32,32]{2,1,0:T(8,128)S(1)} %fusion.2), custom_call_target="InvertDiagBlocksLowerTriangular" | custom-call | tf_op jit(solution)/shard_map/jit(_solve_triangular)/triangular_solve | solution.py:177
  75.9 0.2 fusion.4
  76.2 0.1 concatenate.6.inverse
  76.3 0.4 fusion.1
  76.7 0.1 pad_maximum_fusion.basis
  76.8 8.9 %all-to-all-done.4 = f32[32,1,2304]{2,1,0:T(1,128)S(1)} async-done(((f32[32,1,2304]{2,1,0:T(1,128)}), f32[32,1,2304]{2,1,0:T(1,128)S(1)}, u32[]{:S(2)}, u32[]{:S(2)}) %all-to-all-start.4) | async-done | bytes 294944 | tf_op jit(solution)/shard_map/all_to_all | solution.py:174
  85.7 1.7 %finish.1 = (bf16[256,2304]{1,0:T(8,128)(2,1)}, f32[32,2304]{1,0:T(8,128)}) custom-call(f32[576,128]{1,0:T(8,128)S(1)} %bitcast.28, bf16[32,192]{1,0:T(8,128)(2,1)S(1)} %concatenate.6.inverse, bf16[256,96]{1,0:T(8,128)(2,1)S(1)} %pad_maximum_fusion.basis), custom_call_target="tpu_custom_call" | custom-call | tf_op jit(solution)/shard_map/finish/pallas_call | solution.py:181
  (8 shorter events, 0.2 us)
Async XLA Ops:
  50.2 18.0 %all-to-all-start.3 = ((f32[32,1,2304]{2,1,0:T(1,128)}), f32[32,1,2304]{2,1,0:T(1,128)S(1)}, u32[]{:S(2)}, u32[]{:S(2)}) async-start(f32[32,1,2304]{2,1,0:T(1,128)} %bitcast.4), calls=%async_computation.3 | async-start | bytes 589824 | tf_op jit(solution)/shard_map/all_to_all | solution.py:165
  69.0 16.8 %all-to-all-start.4 = ((f32[32,1,2304]{2,1,0:T(1,128)}), f32[32,1,2304]{2,1,0:T(1,128)S(1)}, u32[]{:S(2)}, u32[]{:S(2)}) async-start(f32[32,1,2304]{2,1,0:T(1,128)} %bitcast.6), calls=%async_computation.4 | async-start | bytes 589824 | tf_op jit(solution)/shard_map/all_to_all | solution.py:174

commit v4 on v3

--- a/solution.py
+++ b/solution.py
@@ -11,6 +11,9 @@
 BITS = ("z2", "z1", "z0", "x1", "x0", "y2", "y1", "y0", "c")
 NEAR = ("x1", "x0", "y0", "c")
 FAR = ("z2", "z1", "z0", "y2", "y1")
+ALONG_DP = ("z2", "z1", "z0", "x1", "x0")
+FIRST_P = ("z2", "z1", "x1", "y2", "y0", "c")
+FIRST_Q = ("z2", "x1")
 ROWS, RANK, COLS, PEERS = 256, 32, 2304, 32
 LANES = 128
 TILES = COLS // LANES
@@ -19,15 +22,17 @@
 F32, BF16 = jnp.float32, jnp.bfloat16
 
 
-def groups_along(bits):
+def groups_along(bits, first):
     ids = np.arange(512).reshape((2,) * 9)
     inner = [i for i, b in enumerate(BITS) if b in bits]
     outer = [i for i, b in enumerate(BITS) if b not in bits]
-    return np.transpose(ids, outer + inner).reshape(-1, 2 ** len(inner)).tolist()
-
-
-def exchange(x, bits):
-    return lax.all_to_all(x, BOTH, 0, 0, axis_index_groups=groups_along(bits))
+    groups = np.transpose(ids, outer + inner).reshape(-1, 2 ** len(inner))
+    start = sum(1 << (len(BITS) - 1 - i) for i in inner if BITS[i] in first)
+    return (groups ^ start).tolist()
+
+
+def exchange(x, bits, first):
+    return lax.all_to_all(x, BOTH, 0, 0, axis_index_groups=groups_along(bits, first))
 
 
 def spread(x, count):
@@ -35,9 +40,10 @@
 
 
 def sum_all(p):
-    part = jnp.sum(exchange(p.reshape(16, p.shape[0] // 16, p.shape[1]), NEAR), axis=0)
-    part = jnp.sum(exchange(spread(part, 32), FAR), axis=0)
-    return exchange(spread(part, 16), NEAR).reshape(p.shape)
+    near, far = 2 ** len(NEAR), 2 ** len(FAR)
+    part = jnp.sum(exchange(p.reshape(near, p.shape[0] // near, p.shape[1]), NEAR, FIRST_P), axis=0)
+    part = jnp.sum(exchange(spread(part, far), FAR, FIRST_P), axis=0)
+    return exchange(spread(part, near), NEAR, FIRST_P).reshape(p.shape)
 
 
 def cut(x, count):
@@ -84,23 +90,29 @@
     p_out[...] = total
 
 
+def tile_rows(k, t):
+    return pl.ds(8 * (k * TILES + t), 8)
+
+
 def partial(p, corrected, out):
     left = jnp.concatenate(cut(p[...], 3), axis=0)
     for t in range(0, TILES, 2):
         acc = dot(left, corrected[:, pl.ds(t * LANES, 2 * LANES)], ((1,), (0,)))
         acc = acc[:RANK] + acc[RANK : 2 * RANK] + acc[2 * RANK :]
         for h in range(2):
-            for k in range(0, RANK, 8):
-                out[pl.ds(k * TILES + t + h, 8, stride=TILES), :] = acc[k : k + 8, h * LANES : (h + 1) * LANES]
+            for k in range(RANK // 8):
+                out[tile_rows(k, t + h), :] = acc[8 * k : 8 * k + 8, h * LANES : (h + 1) * LANES]
 
 
 def gathered(x, out):
-    for t in range(TILES):
-        at = [pl.ds(k * TILES + t, 8, stride=TILES) for k in range(0, PEERS, 8)]
-        acc = (x[at[0], :] + x[at[1], :]) + (x[at[2], :] + x[at[3], :])
-        acc = jnp.broadcast_to(jnp.sum(acc, axis=0, keepdims=True), (8, LANES))
-        for rows in at:
-            out[rows, :] = acc
+    size = 4 * TILES
+    acc = x[pl.ds(0, size), :]
+    for i in range(1, PEERS // 4):
+        acc = acc + x[pl.ds(i * size, size), :]
+    one = (acc[:TILES] + acc[TILES : 2 * TILES]) + (acc[2 * TILES : 3 * TILES] + acc[3 * TILES :])
+    four = jnp.concatenate([one] * 4, axis=0)
+    for i in range(PEERS // 4):
+        out[pl.ds(i * size, size), :] = four
 
 
 def finish(raw, inverse, basis, approx_out, q_out, approx, q_new, sems):
@@ -108,8 +120,7 @@
     for i in range(COLS // WIDE):
         parts = []
         for t in range(i * WIDE // LANES, (i + 1) * WIDE // LANES):
-            rows = [raw[pl.ds(k * TILES + t, 8, stride=TILES), :] for k in range(0, RANK, 8)]
-            parts.append(jnp.concatenate(rows, axis=0))
+            parts.append(jnp.concatenate([raw[tile_rows(k, t), :] for k in range(RANK // 8)], axis=0))
         r1, r2, r3 = cut(jnp.concatenate(parts, axis=1), 3)
         q = dot(inverse[...], jnp.concatenate([r1, r2, r1, r2, r3, r1], axis=0), ((1,), (0,)))
         cols = pl.ds(i * WIDE, WIDE)
@@ -162,7 +173,7 @@
         compiler_params=PARAMS,
         name="partial",
     )(in_vmem(p), in_vmem(corrected))
-    raw = lax.all_to_all(raw.reshape(PEERS, 1, COLS), "dp", 0, 0, tiled=True)
+    raw = exchange(raw.reshape(PEERS, 1, COLS), ALONG_DP, FIRST_Q)
     raw = pl.pallas_call(
         gathered,
         out_shape=pltpu.VMEM(LINEAR, F32),
@@ -171,7 +182,7 @@
         compiler_params=PARAMS,
         name="gathered",
     )(in_vmem(raw.reshape(LINEAR)))
-    raw = lax.all_to_all(raw.reshape(PEERS, 1, COLS), "dp", 0, 0, tiled=True).reshape(LINEAR)
+    raw = exchange(raw.reshape(PEERS, 1, COLS), ALONG_DP, FIRST_Q).reshape(LINEAR)
     gram = dot(p, p, ((1,), (1,)), precision=HIGHEST)
     lower = jnp.linalg.cholesky(gram)
     inverse = jax.scipy.linalg.solve_triangular(lower, jnp.eye(RANK, dtype=F32), lower=True)

time: 87.9 us -> 80.2 us (0.912)
  the two profiles are of different devices: /device:TPU:8 before, /device:TPU:46 now
where the time goes in v4:
time: 80.2 us; the launch traced here: 79.8 us
  blocking collectives  38.5 us (48%)
  starting transfers between devices  16.7 us (21%)
  waiting for transfers between devices  10.3 us (13%)
  other arithmetic  6.87 us (9%)
  Pallas kernels  5.74 us (7%)
    all_to_all x3, blocking collectives, exchange(): lax.all_to_all(x, BOTH, 0, 0, axis_index_groups=groups_along(bits, first))  38.5 us
    all_to_all x2, starting transfers between devices, exchange(): lax.all_to_all(x, BOTH, 0, 0, axis_index_groups=groups_along(bits, first))  16.7 us
    all_to_all x2, waiting for transfers between devices, exchange(): lax.all_to_all(x, BOTH, 0, 0, axis_index_groups=groups_along(bits, first))  10.3 us
    another operation x3, other arithmetic, local(): lower = jnp.linalg.cholesky(gram)  3.6 us
    another operation x2, other arithmetic, local(): jax.scipy.linalg.solve_triangular(lower, jnp.eye(RANK, dtype=F32), lower=...  3.09 us
    pallas_call x1, Pallas kernels, local(): pl.pallas_call(project, out_shape=(pltpu.VMEM((RANK, ROWS), F32), pltpu.V...  2.21 us
    pallas_call x1, Pallas kernels, local(): pl.pallas_call(finish, out_shape=(jax.ShapeDtypeStruct((ROWS, COLS), BF16...  1.73 us
  transfers between devices with their start and end apart: 2, of which 2 were waited for; matrix products, arithmetic and copies ran while one was open for 10% of the time, Pallas kernels for 0%

profile of v4, /device:TPU:46, one launch (start us, length us, event | category | flops | bytes accessed | tf_op | source)
XLA Modules:
  0.0 79.8 jit_solution(8716112862426623781)
XLA Ops:
  0.6 2.2 %project.1 = (f32[32,256]{1,0:T(8,128)S(1)}, bf16[256,2304]{1,0:T(8,128)(2,1)S(1)}) custom-call(bf16[256,2304]{1,0:T(8,128)(2,1)} %bitcast.30, bf16[256,2304]{1,0:T(8,128)(2,1)} %bitcast.31, f32[32,2304]{1,0:T(8,128)} %bitcast.32), custom_call_target="tpu_custom_call" | custom-call | tf_op jit(solution)/shard_map/project/pallas_call | solution.py:153
  2.9 9.0 %all_to_all.25 = f32[16,2,256]{2,1,0:T(2,128)S(1)} all-to-all(f32[16,2,256]{2,1,0:T(2,128)S(1)} %reshape.34), channel_id=1, replica_groups={{35,34,33,32,51,50,49,48,3,2,1,0,19,18,17,16},{39,38,37,36,55,54,53,52,..., dimensions={0} | all-to-all | bytes 65536 | tf_op jit(solution)/shard_map/all_to_all | solution.py:35
  11.9 21.1 %all_to_all.26 = f32[32,2,256]{2,1,0:T(2,128)S(1)} all-to-all(f32[32,2,256]{2,1,0:T(2,128)S(1)} %broadcast_in_dim.10), channel_id=1, replica_groups={{392,396,384,388,456,460,448,452,264,268,256,260,328,332,320,324,136,14..., dimensions={0} | all-to-all | bytes 131072 | tf_op jit(solution)/shard_map/all_to_all | solution.py:35
  33.1 8.4 %all_to_all.27 = f32[16,2,256]{2,1,0:T(2,128)S(1)} all-to-all(f32[16,2,256]{2,1,0:T(2,128)S(1)} %broadcast_in_dim.11), channel_id=1, replica_groups={{35,34,33,32,51,50,49,48,3,2,1,0,19,18,17,16},{39,38,37,36,55,54,53,52,..., dimensions={0} | all-to-all | bytes 65536 | tf_op jit(solution)/shard_map/all_to_all | solution.py:35
  41.5 1.0 %partial.1 = f32[576,128]{1,0:T(8,128)} custom-call(f32[32,256]{1,0:T(8,128)S(1)} %reshape.35.p, bf16[256,2304]{1,0:T(8,128)(2,1)S(1)} %get-tuple-element.7.corrected), custom_call_target="tpu_custom_call" | custom-call | tf_op jit(solution)/shard_map/partial/pallas_call | solution.py:168
  42.5 8.4 %all-to-all-start.3 = ((f32[32,1,2304]{2,1,0:T(1,128)}), f32[32,1,2304]{2,1,0:T(1,128)S(1)}, u32[]{:S(2)}, u32[]{:S(2)}) async-start(f32[32,1,2304]{2,1,0:T(1,128)} %bitcast.4), calls=%async_computation.3 | async-start | bytes 589824 | tf_op jit(solution)/shard_map/all_to_all | solution.py:35
  50.9 0.2 fusion.8
  51.1 0.1 copy.23
  51.2 2.9 %cholesky.17 = f32[32,32]{1,0:T(8,128)S(1)} custom-call(f32[32,32]{1,0:T(8,128)S(1)} %fusion.7), custom_call_target="Cholesky" | custom-call | tf_op jit(solution)/shard_map/jit(cholesky)/cholesky | solution.py:187
  54.1 0.6 compare_reduce_fusion
  54.8 5.6 %all-to-all-done.3 = f32[32,1,2304]{2,1,0:T(1,128)S(1)} async-done(((f32[32,1,2304]{2,1,0:T(1,128)}), f32[32,1,2304]{2,1,0:T(1,128)S(1)}, u32[]{:S(2)}, u32[]{:S(2)}) %all-to-all-start.3) | async-done | bytes 294944 | tf_op jit(solution)/shard_map/all_to_all | solution.py:35
  60.4 0.8 gathered.1
  61.2 8.3 %all-to-all-start.4 = ((f32[32,1,2304]{2,1,0:T(1,128)}), f32[32,1,2304]{2,1,0:T(1,128)S(1)}, u32[]{:S(2)}, u32[]{:S(2)}) async-start(f32[32,1,2304]{2,1,0:T(1,128)} %bitcast.6), calls=%async_computation.4 | async-start | bytes 589824 | tf_op jit(solution)/shard_map/all_to_all | solution.py:35
  69.4 0.7 fusion.2
  70.1 2.4 %custom-call.7 = f32[1,32,32]{1,2,0:T(8,128)S(1)} custom-call(f32[1,32,32]{2,1,0:T(8,128)S(1)} %fusion.2), custom_call_target="InvertDiagBlocksLowerTriangular" | custom-call | tf_op jit(solution)/shard_map/jit(_solve_triangular)/triangular_solve | solution.py:188
  72.5 0.2 fusion.4
  72.8 0.1 concatenate.6.inverse
  72.9 0.4 fusion.1
  73.3 0.1 pad_maximum_fusion.basis
  73.4 4.6 %all-to-all-done.4 = f32[32,1,2304]{2,1,0:T(1,128)S(1)} async-done(((f32[32,1,2304]{2,1,0:T(1,128)}), f32[32,1,2304]{2,1,0:T(1,128)S(1)}, u32[]{:S(2)}, u32[]{:S(2)}) %all-to-all-start.4) | async-done | bytes 294944 | tf_op jit(solution)/shard_map/all_to_all | solution.py:35
  78.0 1.7 %finish.1 = (bf16[256,2304]{1,0:T(8,128)(2,1)}, f32[32,2304]{1,0:T(8,128)}) custom-call(f32[576,128]{1,0:T(8,128)S(1)} %bitcast.28, bf16[32,192]{1,0:T(8,128)(2,1)S(1)} %concatenate.6.inverse, bf16[256,96]{1,0:T(8,128)(2,1)S(1)} %pad_maximum_fusion.basis), custom_call_target="tpu_custom_call" | custom-call | tf_op jit(solution)/shard_map/finish/pallas_call | solution.py:192
  (8 shorter events, 0.2 us)
Async XLA Ops:
  42.5 17.9 %all-to-all-start.3 = ((f32[32,1,2304]{2,1,0:T(1,128)}), f32[32,1,2304]{2,1,0:T(1,128)S(1)}, u32[]{:S(2)}, u32[]{:S(2)}) async-start(f32[32,1,2304]{2,1,0:T(1,128)} %bitcast.4), calls=%async_computation.3 | async-start | bytes 589824 | tf_op jit(solution)/shard_map/all_to_all | solution.py:35
  61.2 16.9 %all-to-all-start.4 = ((f32[32,1,2304]{2,1,0:T(1,128)}), f32[32,1,2304]{2,1,0:T(1,128)S(1)}, u32[]{:S(2)}, u32[]{:S(2)}) async-start(f32[32,1,2304]{2,1,0:T(1,128)} %bitcast.6), calls=%async_computation.4 | async-start | bytes 589824 | tf_op jit(solution)/shard_map/all_to_all | solution.py:35

commit v5 on v4

--- a/solution.py
+++ b/solution.py
@@ -14,7 +14,7 @@
 ALONG_DP = ("z2", "z1", "z0", "x1", "x0")
 FIRST_P = ("z2", "z1", "x1", "y2", "y0", "c")
 FIRST_Q = ("z2", "x1")
-ROWS, RANK, COLS, PEERS = 256, 32, 2304, 32
+ROWS, RANK, COLS, PEERS, N_DP = 256, 32, 2304, 32, 32
 LANES = 128
 TILES = COLS // LANES
 WIDE = 768
@@ -52,15 +52,6 @@
         top = x.astype(BF16)
         out.append(top)
         x = x - top.astype(F32)
-    return out
-
-
-def pieces(x, count):
-    out = []
-    for _ in range(count):
-        top = lax.reduce_precision(x, 8, 7)
-        out.append(top.astype(BF16))
-        x = x - top
     return out
 
 
@@ -104,6 +95,24 @@
                 out[tile_rows(k, t + h), :] = acc[8 * k : 8 * k + 8, h * LANES : (h + 1) * LANES]
 
 
+def factor(p, left):
+    p = p[...]
+    row = lax.broadcasted_iota(jnp.int32, (RANK, 2 * RANK), 0)
+    lane = lax.broadcasted_iota(jnp.int32, (RANK, 2 * RANK), 1)
+    unit = jnp.where(lane == row + RANK, 1.0, 0.0)
+    gram = dot(p, p, ((1,), (1,)), precision=HIGHEST)
+    m = jnp.concatenate([gram, unit[:, RANK:]], axis=1)
+    for k in range(RANK - 1):
+        ratio = m[:, k : k + 1] / m[k : k + 1, k : k + 1]
+        m = m - jnp.where(row > k, ratio, 0.0) * m[k : k + 1, :]
+    pivot = jnp.sum(jnp.where(lane == row, m, 0.0), axis=1, keepdims=True)
+    inverse = m[:, RANK:] / jnp.sqrt(pivot)
+    basis = dot(inverse, p, ((1,), (0,)), precision=HIGHEST)
+    weight = dot(inverse.T, basis, ((1,), (0,)), precision=HIGHEST) * (1.0 / N_DP)
+    t1, t2, t3 = cut(jnp.concatenate([weight.T, inverse], axis=0), 3)
+    left[...] = jnp.concatenate([t1, t1, t2, t2, t1, t3], axis=1)
+
+
 def gathered(x, out):
     size = 4 * TILES
     acc = x[pl.ds(0, size), :]
@@ -115,18 +124,17 @@
         out[pl.ds(i * size, size), :] = four
 
 
-def finish(raw, inverse, basis, approx_out, q_out, approx, q_new, sems):
+def finish(raw, left, approx_out, q_out, approx, q_new, sems):
     pending = []
-    for i in range(COLS // WIDE):
+    for i in range(CHUNKS):
         parts = []
         for t in range(i * WIDE // LANES, (i + 1) * WIDE // LANES):
             parts.append(jnp.concatenate([raw[tile_rows(k, t), :] for k in range(RANK // 8)], axis=0))
         r1, r2, r3 = cut(jnp.concatenate(parts, axis=1), 3)
-        q = dot(inverse[...], jnp.concatenate([r1, r2, r1, r2, r3, r1], axis=0), ((1,), (0,)))
+        both = dot(left[...], jnp.concatenate([r1, r2, r1, r2, r3, r1], axis=0), ((1,), (0,)))
         cols = pl.ds(i * WIDE, WIDE)
-        q_new[:, cols] = q
-        q1, q2 = cut(q, 2)
-        approx[:, cols] = dot(basis[...], jnp.concatenate([q1, q1, q2], axis=0), ((1,), (0,))).astype(BF16)
+        approx[:, cols] = both[:ROWS].astype(BF16)
+        q_new[:, cols] = both[ROWS:]
         for j, (src, dst) in enumerate(((approx, approx_out), (q_new, q_out))):
             copy = pltpu.make_async_copy(src.at[:, cols], dst.at[:, cols], sems.at[i, j])
             copy.start()
@@ -174,6 +182,16 @@
         name="partial",
     )(in_vmem(p), in_vmem(corrected))
     raw = exchange(raw.reshape(PEERS, 1, COLS), ALONG_DP, FIRST_Q)
+    left = pl.pallas_call(
+        factor,
+        out_shape=pltpu.VMEM((ROWS + RANK, 6 * RANK), BF16),
+        in_specs=[VMEM],
+        out_specs=VMEM,
+        compiler_params=PARAMS,
+        cost_estimate=pl.CostEstimate(flops=4_000_000_000, bytes_accessed=0, transcendentals=0),
+        name="factor",
+    )(in_vmem(p))
+    raw, left = lax.optimization_barrier((raw, left))
     raw = pl.pallas_call(
         gathered,
         out_shape=pltpu.VMEM(LINEAR, F32),
@@ -183,16 +201,10 @@
         name="gathered",
     )(in_vmem(raw.reshape(LINEAR)))
     raw = exchange(raw.reshape(PEERS, 1, COLS), ALONG_DP, FIRST_Q).reshape(LINEAR)
-    gram = dot(p, p, ((1,), (1,)), precision=HIGHEST)
-    lower = jnp.linalg.cholesky(gram)
-    inverse = jax.scipy.linalg.solve_triangular(lower, jnp.eye(RANK, dtype=F32), lower=True)
-    basis = dot(p, inverse, ((0,), (1,)), precision=HIGHEST) / lax.axis_size("dp")
-    b1, b2 = pieces(basis, 2)
-    i1, i2, i3 = pieces(inverse, 3)
     approx, q_new = pl.pallas_call(
         finish,
         out_shape=(jax.ShapeDtypeStruct((ROWS, COLS), BF16), jax.ShapeDtypeStruct((RANK, COLS), F32)),
-        in_specs=[VMEM] * 3,
+        in_specs=[VMEM] * 2,
         out_specs=(HBM, HBM),
         scratch_shapes=[
             pltpu.VMEM((ROWS, COLS), BF16),
@@ -201,11 +213,7 @@
         ],
         compiler_params=PARAMS,
         name="finish",
-    )(
-        in_vmem(raw),
-        in_vmem(jnp.concatenate([i1, i1, i2, i2, i1, i3], axis=1)),
-        in_vmem(jnp.concatenate([b1, b2, b1], axis=1)),
-    )
+    )(in_vmem(raw), in_vmem(left))
     return (approx[None], q_new.T[None])
 
 

time: 80.2 us -> 78.9 us (0.984)
  blocking collectives: 38.5 us -> 55.1 us
  starting transfers between devices: 16.7 us -> 8.39 us
  other arithmetic: 6.87 us -> 0.07 us
  waiting for transfers between devices: 10.3 us -> 6.13 us
  Pallas kernels: 5.74 us -> 8.07 us
    all_to_all x3 -> x4, blocking collectives: 38.5 us -> 55.1 us  [exchange(): lax.all_to_all(x, BOTH, 0, 0, axis_index_groups=groups_along(bits, first))]
    all_to_all x2 -> x1, starting transfers between devices: 16.7 us -> 8.39 us  [exchange(): lax.all_to_all(x, BOTH, 0, 0, axis_index_groups=groups_along(bits, first))]
    another operation x5 -> x0, other arithmetic: 6.68 us -> none  [the longest x3 3.6 us: local(): lower = jnp.linalg.cholesky(gram)]
    all_to_all x2 -> x1, waiting for transfers between devices: 10.3 us -> 6.13 us  [exchange(): lax.all_to_all(x, BOTH, 0, 0, axis_index_groups=groups_along(bits, first))]
    pallas_call x0 -> x1, Pallas kernels: none -> 3.36 us  [local(): pl.pallas_call(factor, out_shape=pltpu.VMEM((ROWS + RANK, 6 * RANK), BF16...]
  transfers between devices with their start and end apart: 2 -> 1, of which waited for: 2 -> 1; matrix products, arithmetic and copies ran while one was open for 10% -> 0% of each run, Pallas kernels for 0% -> 4%
where the time goes in v5:
time: 78.9 us; the launch traced here: 78.5 us
  blocking collectives  55.1 us (70%)
  starting transfers between devices  8.39 us (11%)
  Pallas kernels  8.07 us (10%)
  waiting for transfers between devices  6.13 us (8%)
    all_to_all x4, blocking collectives, exchange(): lax.all_to_all(x, BOTH, 0, 0, axis_index_groups=groups_along(bits, first))  55.1 us
    all_to_all x1, starting transfers between devices, exchange(): lax.all_to_all(x, BOTH, 0, 0, axis_index_groups=groups_along(bits, first))  8.39 us
    all_to_all x1, waiting for transfers between devices, exchange(): lax.all_to_all(x, BOTH, 0, 0, axis_index_groups=groups_along(bits, first))  6.13 us
    pallas_call x1, Pallas kernels, local(): pl.pallas_call(factor, out_shape=pltpu.VMEM((ROWS + RANK, 6 * RANK), BF16...  3.36 us
    pallas_call x1, Pallas kernels, local(): pl.pallas_call(project, out_shape=(pltpu.VMEM((RANK, ROWS), F32), pltpu.V...  2.21 us
  transfers between devices with their start and end apart: 1, of which 1 were waited for; matrix products, arithmetic and copies ran while one was open for 0% of the time, Pallas kernels for 4%

profile of v5, /device:TPU:46, one launch (start us, length us, event | category | flops | bytes accessed | tf_op | source)
XLA Modules:
  0.0 78.5 jit_solution(8817570898784381558)
XLA Ops:
  0.6 2.2 %project.1 = (f32[32,256]{1,0:T(8,128)S(1)}, bf16[256,2304]{1,0:T(8,128)(2,1)S(1)}) custom-call(bf16[256,2304]{1,0:T(8,128)(2,1)} %bitcast.16, bf16[256,2304]{1,0:T(8,128)(2,1)} %bitcast.17, f32[32,2304]{1,0:T(8,128)} %bitcast.18), custom_call_target="tpu_custom_call" | custom-call | tf_op jit(solution)/shard_map/project/pallas_call | solution.py:161
  2.9 9.0 %all_to_all.25 = f32[16,2,256]{2,1,0:T(2,128)S(1)} all-to-all(f32[16,2,256]{2,1,0:T(2,128)S(1)} %reshape.24), channel_id=1, replica_groups={{35,34,33,32,51,50,49,48,3,2,1,0,19,18,17,16},{39,38,37,36,55,54,53,52,..., dimensions={0} | all-to-all | bytes 65536 | tf_op jit(solution)/shard_map/all_to_all | solution.py:35
  11.9 21.1 %all_to_all.26 = f32[32,2,256]{2,1,0:T(2,128)S(1)} all-to-all(f32[32,2,256]{2,1,0:T(2,128)S(1)} %broadcast_in_dim.8), channel_id=1, replica_groups={{392,396,384,388,456,460,448,452,264,268,256,260,328,332,320,324,136,14..., dimensions={0} | all-to-all | bytes 131072 | tf_op jit(solution)/shard_map/all_to_all | solution.py:35
  33.1 8.4 %all_to_all.27 = f32[16,2,256]{2,1,0:T(2,128)S(1)} all-to-all(f32[16,2,256]{2,1,0:T(2,128)S(1)} %broadcast_in_dim.9), channel_id=1, replica_groups={{35,34,33,32,51,50,49,48,3,2,1,0,19,18,17,16},{39,38,37,36,55,54,53,52,..., dimensions={0} | all-to-all | bytes 65536 | tf_op jit(solution)/shard_map/all_to_all | solution.py:35
  41.5 1.0 %partial.1 = f32[576,128]{1,0:T(8,128)} custom-call(f32[32,256]{1,0:T(8,128)S(1)} %reshape.25.p, bf16[256,2304]{1,0:T(8,128)(2,1)S(1)} %get-tuple-element.9.corrected), custom_call_target="tpu_custom_call" | custom-call | tf_op jit(solution)/shard_map/partial/pallas_call | solution.py:176
  42.5 8.4 %all-to-all-start.3 = ((f32[32,1,2304]{2,1,0:T(1,128)}), f32[32,1,2304]{2,1,0:T(1,128)S(1)}, u32[]{:S(2)}, u32[]{:S(2)}) async-start(f32[32,1,2304]{2,1,0:T(1,128)} %bitcast.4), calls=%async_computation.3 | async-start | bytes 589824 | tf_op jit(solution)/shard_map/all_to_all | solution.py:35
  50.9 3.4 %factor.1.left = bf16[288,192]{1,0:T(8,128)(2,1)S(1)} custom-call(f32[32,256]{1,0:T(8,128)S(1)} %reshape.25.p), custom_call_target="tpu_custom_call" | custom-call | flops 4000000000 | tf_op jit(solution)/shard_map/factor/pallas_call | solution.py:185
  54.3 6.1 %all-to-all-done.3 = f32[32,1,2304]{2,1,0:T(1,128)S(1)} async-done(((f32[32,1,2304]{2,1,0:T(1,128)}), f32[32,1,2304]{2,1,0:T(1,128)S(1)}, u32[]{:S(2)}, u32[]{:S(2)}) %all-to-all-start.3) | async-done | bytes 294944 | tf_op jit(solution)/shard_map/all_to_all | solution.py:35
  60.4 16.7 %all_to_all.28 = f32[32,1,2304]{2,1,0:T(1,128)S(1)} all-to-all(f32[32,1,2304]{2,1,0:T(1,128)S(1)} %bitcast.15), channel_id=1, replica_groups={{288,304,256,272,352,368,320,336,416,432,384,400,480,496,448,464,32,48,..., dimensions={0} | all-to-all | bytes 589824 | tf_op jit(solution)/shard_map/all_to_all | solution.py:35
  77.1 1.4 %finish.1 = (bf16[256,2304]{1,0:T(8,128)(2,1)}, f32[32,2304]{1,0:T(8,128)}) custom-call(f32[576,128]{1,0:T(8,128)S(1)} %bitcast.14, bf16[288,192]{1,0:T(8,128)(2,1)S(1)} %factor.1.left), custom_call_target="tpu_custom_call" | custom-call | tf_op jit(solution)/shard_map/finish/pallas_call | solution.py:204
  (7 shorter events, 0.2 us)
Async XLA Ops:
  42.5 17.9 %all-to-all-start.3 = ((f32[32,1,2304]{2,1,0:T(1,128)}), f32[32,1,2304]{2,1,0:T(1,128)S(1)}, u32[]{:S(2)}, u32[]{:S(2)}) async-start(f32[32,1,2304]{2,1,0:T(1,128)} %bitcast.4), calls=%async_computation.3 | async-start | bytes 589824 | tf_op jit(solution)/shard_map/all_to_all | solution.py:35

commit v6 on v5

--- a/solution.py
+++ b/solution.py
@@ -22,13 +22,27 @@
 F32, BF16 = jnp.float32, jnp.bfloat16
 
 
+def places():
+    i = np.arange(512)
+    return np.stack([i // 64, i // 16 % 4, i // 2 % 8, i % 2], axis=1)
+
+
 def groups_along(bits, first):
     ids = np.arange(512).reshape((2,) * 9)
     inner = [i for i, b in enumerate(BITS) if b in bits]
     outer = [i for i, b in enumerate(BITS) if b not in bits]
     groups = np.transpose(ids, outer + inner).reshape(-1, 2 ** len(inner))
     start = sum(1 << (len(BITS) - 1 - i) for i in inner if BITS[i] in first)
-    return (groups ^ start).tolist()
+    at, size = places(), np.array([8, 4, 8, 2])
+    listed = []
+    for group in groups:
+        root = group[0] ^ start
+        apart = np.abs(at[group] - at[root])
+        hops = np.minimum(apart, size - apart) @ np.array([4, 4, 4, 1])
+        order = np.argsort(-hops, kind="stable")
+        rest = [int(m) for m in group[order] if m != root]
+        listed.append([int(root)] + rest)
+    return listed
 
 
 def exchange(x, bits, first):

time: 78.9 us -> 78.4 us (level)
  the two profiles are of different devices: /device:TPU:46 before, /device:TPU:40 now
where the time goes in v6:
time: 78.4 us; the launch traced here: 78.1 us
  blocking collectives  55.2 us (70%)
  starting transfers between devices  10.2 us (13%)
  Pallas kernels  8.07 us (10%)
  waiting for transfers between devices  3.73 us (5%)
    all_to_all x4, blocking collectives, exchange(): lax.all_to_all(x, BOTH, 0, 0, axis_index_groups=groups_along(bits, first))  55.2 us
    all_to_all x1, starting transfers between devices, exchange(): lax.all_to_all(x, BOTH, 0, 0, axis_index_groups=groups_along(bits, first))  10.2 us
    all_to_all x1, waiting for transfers between devices, exchange(): lax.all_to_all(x, BOTH, 0, 0, axis_index_groups=groups_along(bits, first))  3.73 us
    pallas_call x1, Pallas kernels, local(): pl.pallas_call(factor, out_shape=pltpu.VMEM((ROWS + RANK, 6 * RANK), BF16...  3.36 us
    pallas_call x1, Pallas kernels, local(): pl.pallas_call(project, out_shape=(pltpu.VMEM((RANK, ROWS), F32), pltpu.V...  2.21 us
  transfers between devices with their start and end apart: 1, of which 1 were waited for; matrix products, arithmetic and copies ran while one was open for 0% of the time, Pallas kernels for 4%

profile of v6, /device:TPU:40, one launch (start us, length us, event | category | flops | bytes accessed | tf_op | source)
XLA Modules:
  0.0 78.1 jit_solution(4686277673694965203)
XLA Ops:
  0.6 2.2 %project.1 = (f32[32,256]{1,0:T(8,128)S(1)}, bf16[256,2304]{1,0:T(8,128)(2,1)S(1)}) custom-call(bf16[256,2304]{1,0:T(8,128)(2,1)} %bitcast.16, bf16[256,2304]{1,0:T(8,128)(2,1)} %bitcast.17, f32[32,2304]{1,0:T(8,128)} %bitcast.18), custom_call_target="tpu_custom_call" | custom-call | tf_op jit(solution)/shard_map/project/pallas_call | solution.py:175
  2.9 9.2 %all_to_all.25 = f32[16,2,256]{2,1,0:T(2,128)S(1)} all-to-all(f32[16,2,256]{2,1,0:T(2,128)S(1)} %reshape.24), channel_id=1, replica_groups={{35,0,1,2,16,48,3,17,49,18,32,50,19,33,51,34},{39,4,5,6,20,52,7,21,53,2..., dimensions={0} | all-to-all | bytes 65536 | tf_op jit(solution)/shard_map/all_to_all | solution.py:49
  12.1 21.1 %all_to_all.26 = f32[32,2,256]{2,1,0:T(2,128)S(1)} all-to-all(f32[32,2,256]{2,1,0:T(2,128)S(1)} %broadcast_in_dim.8), channel_id=1, replica_groups={{392,128,64,192,0,132,140,256,68,76,196,204,320,448,4,12,136,260,268,38..., dimensions={0} | all-to-all | bytes 131072 | tf_op jit(solution)/shard_map/all_to_all | solution.py:49
  33.2 8.4 %all_to_all.27 = f32[16,2,256]{2,1,0:T(2,128)S(1)} all-to-all(f32[16,2,256]{2,1,0:T(2,128)S(1)} %broadcast_in_dim.9), channel_id=1, replica_groups={{35,0,1,2,16,48,3,17,49,18,32,50,19,33,51,34},{39,4,5,6,20,52,7,21,53,2..., dimensions={0} | all-to-all | bytes 65536 | tf_op jit(solution)/shard_map/all_to_all | solution.py:49
  41.7 1.0 %partial.1 = f32[576,128]{1,0:T(8,128)} custom-call(f32[32,256]{1,0:T(8,128)S(1)} %reshape.25.p, bf16[256,2304]{1,0:T(8,128)(2,1)S(1)} %get-tuple-element.9.corrected), custom_call_target="tpu_custom_call" | custom-call | tf_op jit(solution)/shard_map/partial/pallas_call | solution.py:190
  42.7 10.2 %all-to-all-start.3 = ((f32[32,1,2304]{2,1,0:T(1,128)}), f32[32,1,2304]{2,1,0:T(1,128)S(1)}, u32[]{:S(2)}, u32[]{:S(2)}) async-start(f32[32,1,2304]{2,1,0:T(1,128)} %bitcast.4), calls=%async_computation.3 | async-start | bytes 589824 | tf_op jit(solution)/shard_map/all_to_all | solution.py:49
  53.0 3.4 %factor.1.left = bf16[288,192]{1,0:T(8,128)(2,1)S(1)} custom-call(f32[32,256]{1,0:T(8,128)S(1)} %reshape.25.p), custom_call_target="tpu_custom_call" | custom-call | flops 4000000000 | tf_op jit(solution)/shard_map/factor/pallas_call | solution.py:199
  56.3 3.7 %all-to-all-done.3 = f32[32,1,2304]{2,1,0:T(1,128)S(1)} async-done(((f32[32,1,2304]{2,1,0:T(1,128)}), f32[32,1,2304]{2,1,0:T(1,128)S(1)}, u32[]{:S(2)}, u32[]{:S(2)}) %all-to-all-start.3) | async-done | bytes 294944 | tf_op jit(solution)/shard_map/all_to_all | solution.py:49
  60.1 16.6 %all_to_all.28 = f32[32,1,2304]{2,1,0:T(1,128)S(1)} all-to-all(f32[32,1,2304]{2,1,0:T(1,128)S(1)} %bitcast.15), channel_id=1, replica_groups={{288,0,16,48,64,448,32,80,112,128,384,464,496,96,144,176,192,320,400,43..., dimensions={0} | all-to-all | bytes 589824 | tf_op jit(solution)/shard_map/all_to_all | solution.py:49
  76.7 1.4 %finish.1 = (bf16[256,2304]{1,0:T(8,128)(2,1)}, f32[32,2304]{1,0:T(8,128)}) custom-call(f32[576,128]{1,0:T(8,128)S(1)} %bitcast.14, bf16[288,192]{1,0:T(8,128)(2,1)S(1)} %factor.1.left), custom_call_target="tpu_custom_call" | custom-call | tf_op jit(solution)/shard_map/finish/pallas_call | solution.py:218
  (7 shorter events, 0.2 us)
Async XLA Ops:
  42.7 17.3 %all-to-all-start.3 = ((f32[32,1,2304]{2,1,0:T(1,128)}), f32[32,1,2304]{2,1,0:T(1,128)S(1)}, u32[]{:S(2)}, u32[]{:S(2)}) async-start(f32[32,1,2304]{2,1,0:T(1,128)} %bitcast.4), calls=%async_computation.3 | async-start | bytes 589824 | tf_op jit(solution)/shard_map/all_to_all | solution.py:49

commit v7 on v6

--- a/solution.py
+++ b/solution.py
@@ -13,7 +13,8 @@
 FAR = ("z2", "z1", "z0", "y2", "y1")
 ALONG_DP = ("z2", "z1", "z0", "x1", "x0")
 FIRST_P = ("z2", "z1", "x1", "y2", "y0", "c")
-FIRST_Q = ("z2", "x1")
+FIRST_SCATTER = ('z2', 'z0', 'x1')
+FIRST_GATHER = ('z2', 'x1')
 ROWS, RANK, COLS, PEERS, N_DP = 256, 32, 2304, 32, 32
 LANES = 128
 TILES = COLS // LANES
@@ -27,7 +28,7 @@
     return np.stack([i // 64, i // 16 % 4, i // 2 % 8, i % 2], axis=1)
 
 
-def groups_along(bits, first):
+def groups_along(bits, first, far=True):
     ids = np.arange(512).reshape((2,) * 9)
     inner = [i for i, b in enumerate(BITS) if b in bits]
     outer = [i for i, b in enumerate(BITS) if b not in bits]
@@ -39,14 +40,14 @@
         root = group[0] ^ start
         apart = np.abs(at[group] - at[root])
         hops = np.minimum(apart, size - apart) @ np.array([4, 4, 4, 1])
-        order = np.argsort(-hops, kind="stable")
+        order = np.argsort(-hops if far else hops, kind="stable")
         rest = [int(m) for m in group[order] if m != root]
         listed.append([int(root)] + rest)
     return listed
 
 
-def exchange(x, bits, first):
-    return lax.all_to_all(x, BOTH, 0, 0, axis_index_groups=groups_along(bits, first))
+def exchange(x, bits, first, far=True):
+    return lax.all_to_all(x, BOTH, 0, 0, axis_index_groups=groups_along(bits, first, far))
 
 
 def spread(x, count):
@@ -55,9 +56,9 @@
 
 def sum_all(p):
     near, far = 2 ** len(NEAR), 2 ** len(FAR)
-    part = jnp.sum(exchange(p.reshape(near, p.shape[0] // near, p.shape[1]), NEAR, FIRST_P), axis=0)
-    part = jnp.sum(exchange(spread(part, far), FAR, FIRST_P), axis=0)
-    return exchange(spread(part, near), NEAR, FIRST_P).reshape(p.shape)
+    part = jnp.sum(exchange(p.reshape(near, p.shape[0] // near, p.shape[1]), NEAR, FIRST_P, far=False), axis=0)
+    part = jnp.sum(exchange(spread(part, far), FAR, FIRST_P, far=True), axis=0)
+    return exchange(spread(part, near), NEAR, FIRST_P, far=False).reshape(p.shape)
 
 
 def cut(x, count):
@@ -99,14 +100,27 @@
     return pl.ds(8 * (k * TILES + t), 8)
 
 
+def slots():
+    scatter = groups_along(ALONG_DP, FIRST_SCATTER, far=True)[0]
+    gather = groups_along(ALONG_DP, FIRST_GATHER, far=True)[0]
+    return [scatter.index(member) for member in gather]
+
+
 def partial(p, corrected, out):
     left = jnp.concatenate(cut(p[...], 3), axis=0)
+    place = slots()
     for t in range(0, TILES, 2):
         acc = dot(left, corrected[:, pl.ds(t * LANES, 2 * LANES)], ((1,), (0,)))
         acc = acc[:RANK] + acc[RANK : 2 * RANK] + acc[2 * RANK :]
         for h in range(2):
             for k in range(RANK // 8):
-                out[tile_rows(k, t + h), :] = acc[8 * k : 8 * k + 8, h * LANES : (h + 1) * LANES]
+                row, end = 8 * (k * TILES + t + h), 8 * (k * TILES + t + h) + 8
+                while row < end:
+                    chunk, at = divmod(row, TILES)
+                    size = min(end - row, TILES - at)
+                    first = 8 * k + 8 - (end - row)
+                    out[pl.ds(place[chunk] * TILES + at, size), :] = acc[first : first + size, h * LANES : (h + 1) * LANES]
+                    row += size
 
 
 def factor(p, left):
@@ -195,7 +209,7 @@
         compiler_params=PARAMS,
         name="partial",
     )(in_vmem(p), in_vmem(corrected))
-    raw = exchange(raw.reshape(PEERS, 1, COLS), ALONG_DP, FIRST_Q)
+    raw = exchange(raw.reshape(PEERS, 1, COLS), ALONG_DP, FIRST_SCATTER, far=True)
     left = pl.pallas_call(
         factor,
         out_shape=pltpu.VMEM((ROWS + RANK, 6 * RANK), BF16),
@@ -214,7 +228,7 @@
         compiler_params=PARAMS,
         name="gathered",
     )(in_vmem(raw.reshape(LINEAR)))
-    raw = exchange(raw.reshape(PEERS, 1, COLS), ALONG_DP, FIRST_Q).reshape(LINEAR)
+    raw = exchange(raw.reshape(PEERS, 1, COLS), ALONG_DP, FIRST_GATHER, far=True).reshape(LINEAR)
     approx, q_new = pl.pallas_call(
         finish,
         out_shape=(jax.ShapeDtypeStruct((ROWS, COLS), BF16), jax.ShapeDtypeStruct((RANK, COLS), F32)),

time: 78.4 us -> 78.1 us (level)
  waiting for transfers between devices: 3.73 us -> 4.72 us
    all_to_all x1, waiting for transfers between devices: 3.73 us -> 4.72 us  [exchange(): lax.all_to_all(x, BOTH, 0, 0, axis_index_groups=groups_along(bits, first,...]
where the time goes in v7:
time: 78.1 us; the launch traced here: 77.8 us
  blocking collectives  54.6 us (70%)
  starting transfers between devices  9.55 us (12%)
  Pallas kernels  8.07 us (10%)
  waiting for transfers between devices  4.72 us (6%)
    all_to_all x4, blocking collectives, exchange(): lax.all_to_all(x, BOTH, 0, 0, axis_index_groups=groups_along(bits, first,...  54.6 us
    all_to_all x1, starting transfers between devices, exchange(): lax.all_to_all(x, BOTH, 0, 0, axis_index_groups=groups_along(bits, first,...  9.55 us
    all_to_all x1, waiting for transfers between devices, exchange(): lax.all_to_all(x, BOTH, 0, 0, axis_index_groups=groups_along(bits, first,...  4.72 us
    pallas_call x1, Pallas kernels, local(): pl.pallas_call(factor, out_shape=pltpu.VMEM((ROWS + RANK, 6 * RANK), BF16...  3.36 us
    pallas_call x1, Pallas kernels, local(): pl.pallas_call(project, out_shape=(pltpu.VMEM((RANK, ROWS), F32), pltpu.V...  2.21 us
  transfers between devices with their start and end apart: 1, of which 1 were waited for; matrix products, arithmetic and copies ran while one was open for 0% of the time, Pallas kernels for 4%

profile of v7, /device:TPU:40, one launch (start us, length us, event | category | flops | bytes accessed | tf_op | source)
XLA Modules:
  0.0 77.8 jit_solution(4022301726906509099)
XLA Ops:
  0.6 2.2 %project.1 = (f32[32,256]{1,0:T(8,128)S(1)}, bf16[256,2304]{1,0:T(8,128)(2,1)S(1)}) custom-call(bf16[256,2304]{1,0:T(8,128)(2,1)} %bitcast.16, bf16[256,2304]{1,0:T(8,128)(2,1)} %bitcast.17, f32[32,2304]{1,0:T(8,128)} %bitcast.18), custom_call_target="tpu_custom_call" | custom-call | tf_op jit(solution)/shard_map/project/pallas_call | solution.py:189
  2.9 9.2 %all_to_all.25 = f32[16,2,256]{2,1,0:T(2,128)S(1)} all-to-all(f32[16,2,256]{2,1,0:T(2,128)S(1)} %reshape.24), channel_id=1, replica_groups={{35,34,19,33,51,18,32,50,3,17,49,2,16,48,1,0},{39,38,23,37,55,22,36,54,..., dimensions={0} | all-to-all | bytes 65536 | tf_op jit(solution)/shard_map/all_to_all | solution.py:50
  12.1 21.1 %all_to_all.26 = f32[32,2,256]{2,1,0:T(2,128)S(1)} all-to-all(f32[32,2,256]{2,1,0:T(2,128)S(1)} %broadcast_in_dim.8), channel_id=1, replica_groups={{392,128,64,192,0,132,140,256,68,76,196,204,320,448,4,12,136,260,268,38..., dimensions={0} | all-to-all | bytes 131072 | tf_op jit(solution)/shard_map/all_to_all | solution.py:50
  33.2 8.4 %all_to_all.27 = f32[16,2,256]{2,1,0:T(2,128)S(1)} all-to-all(f32[16,2,256]{2,1,0:T(2,128)S(1)} %broadcast_in_dim.9), channel_id=1, replica_groups={{35,34,19,33,51,18,32,50,3,17,49,2,16,48,1,0},{39,38,23,37,55,22,36,54,..., dimensions={0} | all-to-all | bytes 65536 | tf_op jit(solution)/shard_map/all_to_all | solution.py:50
  41.7 1.0 %partial.1 = f32[576,128]{1,0:T(8,128)} custom-call(f32[32,256]{1,0:T(8,128)S(1)} %reshape.25.p, bf16[256,2304]{1,0:T(8,128)(2,1)S(1)} %get-tuple-element.9.corrected), custom_call_target="tpu_custom_call" | custom-call | tf_op jit(solution)/shard_map/partial/pallas_call | solution.py:204
  42.7 9.6 %all-to-all-start.3 = ((f32[32,1,2304]{2,1,0:T(1,128)}), f32[32,1,2304]{2,1,0:T(1,128)S(1)}, u32[]{:S(2)}, u32[]{:S(2)}) async-start(f32[32,1,2304]{2,1,0:T(1,128)} %bitcast.4), calls=%async_computation.3 | async-start | bytes 589824 | tf_op jit(solution)/shard_map/all_to_all | solution.py:50
  52.3 3.4 %factor.1.left = bf16[288,192]{1,0:T(8,128)(2,1)S(1)} custom-call(f32[32,256]{1,0:T(8,128)S(1)} %reshape.25.p), custom_call_target="tpu_custom_call" | custom-call | flops 4000000000 | tf_op jit(solution)/shard_map/factor/pallas_call | solution.py:213
  55.7 4.7 %all-to-all-done.3 = f32[32,1,2304]{2,1,0:T(1,128)S(1)} async-done(((f32[32,1,2304]{2,1,0:T(1,128)}), f32[32,1,2304]{2,1,0:T(1,128)S(1)}, u32[]{:S(2)}, u32[]{:S(2)}) %all-to-all-start.3) | async-done | bytes 294944 | tf_op jit(solution)/shard_map/all_to_all | solution.py:50
  60.4 16.0 %all_to_all.28 = f32[32,1,2304]{2,1,0:T(1,128)S(1)} all-to-all(f32[32,1,2304]{2,1,0:T(1,128)S(1)} %bitcast.15), channel_id=1, replica_groups={{288,0,16,48,64,448,32,80,112,128,384,464,496,96,144,176,192,320,400,43..., dimensions={0} | all-to-all | bytes 589824 | tf_op jit(solution)/shard_map/all_to_all | solution.py:50
  76.4 1.4 %finish.1 = (bf16[256,2304]{1,0:T(8,128)(2,1)}, f32[32,2304]{1,0:T(8,128)}) custom-call(f32[576,128]{1,0:T(8,128)S(1)} %bitcast.14, bf16[288,192]{1,0:T(8,128)(2,1)S(1)} %factor.1.left), custom_call_target="tpu_custom_call" | custom-call | tf_op jit(solution)/shard_map/finish/pallas_call | solution.py:232
  (7 shorter events, 0.2 us)
Async XLA Ops:
  42.7 17.6 %all-to-all-start.3 = ((f32[32,1,2304]{2,1,0:T(1,128)}), f32[32,1,2304]{2,1,0:T(1,128)S(1)}, u32[]{:S(2)}, u32[]{:S(2)}) async-start(f32[32,1,2304]{2,1,0:T(1,128)} %bitcast.4), calls=%async_computation.3 | async-start | bytes 589824 | tf_op jit(solution)/shard_map/all_to_all | solution.py:50

commit v8 on v7

--- a/solution.py
+++ b/solution.py
@@ -19,6 +19,7 @@
 LANES = 128
 TILES = COLS // LANES
 WIDE = 768
+READ = 1152
 LIMIT = 12 * 1024 * 1024
 F32, BF16 = jnp.float32, jnp.bfloat16
 
@@ -76,20 +77,20 @@
 
 def project(grad, error, q_init, p_out, corrected, g, e, q, sems):
     def copies(i):
-        cols = pl.ds(i * WIDE, WIDE)
+        cols = pl.ds(i * READ, READ)
         return [
             pltpu.make_async_copy(src.at[:, cols], dst.at[:, cols], sems.at[i, j])
             for j, (src, dst) in enumerate(((grad, g), (error, e), (q_init, q)))
         ]
 
-    for i in range(COLS // WIDE):
+    for i in range(COLS // READ):
         for copy in copies(i):
             copy.start()
     total = jnp.zeros((RANK, ROWS), F32)
-    for i in range(COLS // WIDE):
+    for i in range(COLS // READ):
         for copy in copies(i):
             copy.wait()
-        cols = pl.ds(i * WIDE, WIDE)
+        cols = pl.ds(i * READ, READ)
         both = (g[:, cols].astype(F32) + e[:, cols].astype(F32)).astype(BF16)
         corrected[:, cols] = both
         total = total + dot(q[:, cols].astype(BF16), both, ((1,), (1,)))
@@ -195,7 +196,7 @@
             pltpu.VMEM((ROWS, COLS), BF16),
             pltpu.VMEM((ROWS, COLS), BF16),
             pltpu.VMEM((RANK, COLS), F32),
-            pltpu.SemaphoreType.DMA((CHUNKS, 3)),
+            pltpu.SemaphoreType.DMA((COLS // READ, 3)),
         ],
         compiler_params=PARAMS,
         name="project",

time: 78.1 us -> 78.1 us (level)
  no operation moved by 1% of the time
where the time goes in v8:
time: 78.1 us; the launch traced here: 77.8 us
  blocking collectives  54.6 us (70%)
  starting transfers between devices  9.55 us (12%)
  Pallas kernels  8.03 us (10%)
  waiting for transfers between devices  4.72 us (6%)
    all_to_all x4, blocking collectives, exchange(): lax.all_to_all(x, BOTH, 0, 0, axis_index_groups=groups_along(bits, first,...  54.6 us
    all_to_all x1, starting transfers between devices, exchange(): lax.all_to_all(x, BOTH, 0, 0, axis_index_groups=groups_along(bits, first,...  9.55 us
    all_to_all x1, waiting for transfers between devices, exchange(): lax.all_to_all(x, BOTH, 0, 0, axis_index_groups=groups_along(bits, first,...  4.72 us
    pallas_call x1, Pallas kernels, local(): pl.pallas_call(factor, out_shape=pltpu.VMEM((ROWS + RANK, 6 * RANK), BF16...  3.36 us
    pallas_call x1, Pallas kernels, local(): pl.pallas_call(project, out_shape=(pltpu.VMEM((RANK, ROWS), F32), pltpu.V...  2.17 us
  transfers between devices with their start and end apart: 1, of which 1 were waited for; matrix products, arithmetic and copies ran while one was open for 0% of the time, Pallas kernels for 4%

profile of v8, /device:TPU:40, one launch (start us, length us, event | category | flops | bytes accessed | tf_op | source)
XLA Modules:
  0.0 77.8 jit_solution(17601806778919144690)
XLA Ops:
  0.6 2.2 %project.1 = (f32[32,256]{1,0:T(8,128)S(1)}, bf16[256,2304]{1,0:T(8,128)(2,1)S(1)}) custom-call(bf16[256,2304]{1,0:T(8,128)(2,1)} %bitcast.16, bf16[256,2304]{1,0:T(8,128)(2,1)} %bitcast.17, f32[32,2304]{1,0:T(8,128)} %bitcast.18), custom_call_target="tpu_custom_call" | custom-call | tf_op jit(solution)/shard_map/project/pallas_call | solution.py:190
  2.8 9.2 %all_to_all.25 = f32[16,2,256]{2,1,0:T(2,128)S(1)} all-to-all(f32[16,2,256]{2,1,0:T(2,128)S(1)} %reshape.24), channel_id=1, replica_groups={{35,34,19,33,51,18,32,50,3,17,49,2,16,48,1,0},{39,38,23,37,55,22,36,54,..., dimensions={0} | all-to-all | bytes 65536 | tf_op jit(solution)/shard_map/all_to_all | solution.py:51
  12.0 21.1 %all_to_all.26 = f32[32,2,256]{2,1,0:T(2,128)S(1)} all-to-all(f32[32,2,256]{2,1,0:T(2,128)S(1)} %broadcast_in_dim.8), channel_id=1, replica_groups={{392,128,64,192,0,132,140,256,68,76,196,204,320,448,4,12,136,260,268,38..., dimensions={0} | all-to-all | bytes 131072 | tf_op jit(solution)/shard_map/all_to_all | solution.py:51
  33.2 8.4 %all_to_all.27 = f32[16,2,256]{2,1,0:T(2,128)S(1)} all-to-all(f32[16,2,256]{2,1,0:T(2,128)S(1)} %broadcast_in_dim.9), channel_id=1, replica_groups={{35,34,19,33,51,18,32,50,3,17,49,2,16,48,1,0},{39,38,23,37,55,22,36,54,..., dimensions={0} | all-to-all | bytes 65536 | tf_op jit(solution)/shard_map/all_to_all | solution.py:51
  41.6 1.0 %partial.1 = f32[576,128]{1,0:T(8,128)} custom-call(f32[32,256]{1,0:T(8,128)S(1)} %reshape.25.p, bf16[256,2304]{1,0:T(8,128)(2,1)S(1)} %get-tuple-element.9.corrected), custom_call_target="tpu_custom_call" | custom-call | tf_op jit(solution)/shard_map/partial/pallas_call | solution.py:205
  42.7 9.6 %all-to-all-start.3 = ((f32[32,1,2304]{2,1,0:T(1,128)}), f32[32,1,2304]{2,1,0:T(1,128)S(1)}, u32[]{:S(2)}, u32[]{:S(2)}) async-start(f32[32,1,2304]{2,1,0:T(1,128)} %bitcast.4), calls=%async_computation.3 | async-start | bytes 589824 | tf_op jit(solution)/shard_map/all_to_all | solution.py:51
  52.2 3.4 %factor.1.left = bf16[288,192]{1,0:T(8,128)(2,1)S(1)} custom-call(f32[32,256]{1,0:T(8,128)S(1)} %reshape.25.p), custom_call_target="tpu_custom_call" | custom-call | flops 4000000000 | tf_op jit(solution)/shard_map/factor/pallas_call | solution.py:214
  55.6 4.7 %all-to-all-done.3 = f32[32,1,2304]{2,1,0:T(1,128)S(1)} async-done(((f32[32,1,2304]{2,1,0:T(1,128)}), f32[32,1,2304]{2,1,0:T(1,128)S(1)}, u32[]{:S(2)}, u32[]{:S(2)}) %all-to-all-start.3) | async-done | bytes 294944 | tf_op jit(solution)/shard_map/all_to_all | solution.py:51
  60.4 16.0 %all_to_all.28 = f32[32,1,2304]{2,1,0:T(1,128)S(1)} all-to-all(f32[32,1,2304]{2,1,0:T(1,128)S(1)} %bitcast.15), channel_id=1, replica_groups={{288,0,16,48,64,448,32,80,112,128,384,464,496,96,144,176,192,320,400,43..., dimensions={0} | all-to-all | bytes 589824 | tf_op jit(solution)/shard_map/all_to_all | solution.py:51
  76.3 1.4 %finish.1 = (bf16[256,2304]{1,0:T(8,128)(2,1)}, f32[32,2304]{1,0:T(8,128)}) custom-call(f32[576,128]{1,0:T(8,128)S(1)} %bitcast.14, bf16[288,192]{1,0:T(8,128)(2,1)S(1)} %factor.1.left), custom_call_target="tpu_custom_call" | custom-call | tf_op jit(solution)/shard_map/finish/pallas_call | solution.py:233
  (7 shorter events, 0.2 us)
Async XLA Ops:
  42.7 17.6 %all-to-all-start.3 = ((f32[32,1,2304]{2,1,0:T(1,128)}), f32[32,1,2304]{2,1,0:T(1,128)S(1)}, u32[]{:S(2)}, u32[]{:S(2)}) async-start(f32[32,1,2304]{2,1,0:T(1,128)} %bitcast.4), calls=%async_computation.3 | async-start | bytes 589824 | tf_op jit(solution)/shard_map/all_to_all | solution.py:51

commit v9 on v7

--- a/solution.py
+++ b/solution.py
@@ -210,6 +210,7 @@
         name="partial",
     )(in_vmem(p), in_vmem(corrected))
     raw = exchange(raw.reshape(PEERS, 1, COLS), ALONG_DP, FIRST_SCATTER, far=True)
+    raw, p = lax.optimization_barrier((raw, p))
     left = pl.pallas_call(
         factor,
         out_shape=pltpu.VMEM((ROWS + RANK, 6 * RANK), BF16),
@@ -219,7 +220,6 @@
         cost_estimate=pl.CostEstimate(flops=4_000_000_000, bytes_accessed=0, transcendentals=0),
         name="factor",
     )(in_vmem(p))
-    raw, left = lax.optimization_barrier((raw, left))
     raw = pl.pallas_call(
         gathered,
         out_shape=pltpu.VMEM(LINEAR, F32),

time: 78.1 us -> 78.1 us (level)
  waiting for transfers between devices: 4.72 us -> 2.84 us
  blocking collectives: 54.6 us -> 56.1 us
    all_to_all x1, waiting for transfers between devices: 4.72 us -> 2.84 us  [exchange(): lax.all_to_all(x, BOTH, 0, 0, axis_index_groups=groups_along(bits, first,...]
    all_to_all x4, blocking collectives: 54.6 us -> 56.1 us  [exchange(): lax.all_to_all(x, BOTH, 0, 0, axis_index_groups=groups_along(bits, first,...]
where the time goes in v9:
time: 78.1 us; the launch traced here: 77.8 us
  blocking collectives  56.1 us (72%)
  starting transfers between devices  9.96 us (13%)
  Pallas kernels  8.05 us (10%)
  waiting for transfers between devices  2.84 us (4%)
    all_to_all x4, blocking collectives, exchange(): lax.all_to_all(x, BOTH, 0, 0, axis_index_groups=groups_along(bits, first,...  56.1 us
    all_to_all x1, starting transfers between devices, exchange(): lax.all_to_all(x, BOTH, 0, 0, axis_index_groups=groups_along(bits, first,...  9.96 us
    pallas_call x1, Pallas kernels, local(): pl.pallas_call(factor, out_shape=pltpu.VMEM((ROWS + RANK, 6 * RANK), BF16...  3.36 us
    all_to_all x1, waiting for transfers between devices, exchange(): lax.all_to_all(x, BOTH, 0, 0, axis_index_groups=groups_along(bits, first,...  2.84 us
    pallas_call x1, Pallas kernels, local(): pl.pallas_call(project, out_shape=(pltpu.VMEM((RANK, ROWS), F32), pltpu.V...  2.21 us
  transfers between devices with their start and end apart: 1, of which 1 were waited for; matrix products, arithmetic and copies ran while one was open for 0% of the time, Pallas kernels for 4%

profile of v9, /device:TPU:40, one launch (start us, length us, event | category | flops | bytes accessed | tf_op | source)
XLA Modules:
  0.0 77.8 jit_solution(3459010599279860592)
XLA Ops:
  0.6 2.2 %project.1 = (f32[32,256]{1,0:T(8,128)S(1)}, bf16[256,2304]{1,0:T(8,128)(2,1)S(1)}) custom-call(bf16[256,2304]{1,0:T(8,128)(2,1)} %bitcast.16, bf16[256,2304]{1,0:T(8,128)(2,1)} %bitcast.17, f32[32,2304]{1,0:T(8,128)} %bitcast.18), custom_call_target="tpu_custom_call" | custom-call | tf_op jit(solution)/shard_map/project/pallas_call | solution.py:189
  2.9 9.2 %all_to_all.25 = f32[16,2,256]{2,1,0:T(2,128)S(1)} all-to-all(f32[16,2,256]{2,1,0:T(2,128)S(1)} %reshape.24), channel_id=1, replica_groups={{35,34,19,33,51,18,32,50,3,17,49,2,16,48,1,0},{39,38,23,37,55,22,36,54,..., dimensions={0} | all-to-all | bytes 65536 | tf_op jit(solution)/shard_map/all_to_all | solution.py:50
  12.1 21.1 %all_to_all.26 = f32[32,2,256]{2,1,0:T(2,128)S(1)} all-to-all(f32[32,2,256]{2,1,0:T(2,128)S(1)} %broadcast_in_dim.8), channel_id=1, replica_groups={{392,128,64,192,0,132,140,256,68,76,196,204,320,448,4,12,136,260,268,38..., dimensions={0} | all-to-all | bytes 131072 | tf_op jit(solution)/shard_map/all_to_all | solution.py:50
  33.2 8.4 %all_to_all.27 = f32[16,2,256]{2,1,0:T(2,128)S(1)} all-to-all(f32[16,2,256]{2,1,0:T(2,128)S(1)} %broadcast_in_dim.9), channel_id=1, replica_groups={{35,34,19,33,51,18,32,50,3,17,49,2,16,48,1,0},{39,38,23,37,55,22,36,54,..., dimensions={0} | all-to-all | bytes 65536 | tf_op jit(solution)/shard_map/all_to_all | solution.py:50
  41.7 0.3 partial.1
  42.0 17.4 %all_to_all.28 = f32[32,1,2304]{2,1,0:T(1,128)S(1)} all-to-all(f32[32,1,2304]{2,1,0:T(1,128)S(1)} %bitcast.15), channel_id=1, replica_groups={{352,64,0,80,112,128,16,48,96,144,176,192,448,32,160,208,240,256,384,46..., dimensions={0} | all-to-all | bytes 589824 | tf_op jit(solution)/shard_map/all_to_all | solution.py:50
  59.4 0.8 gathered.1
  60.2 10.0 %all-to-all-start.4 = ((f32[32,1,2304]{2,1,0:T(1,128)}), f32[32,1,2304]{2,1,0:T(1,128)S(1)}, u32[]{:S(2)}, u32[]{:S(2)}) async-start(f32[32,1,2304]{2,1,0:T(1,128)} %bitcast.6), calls=%async_computation.4 | async-start | bytes 589824 | tf_op jit(solution)/shard_map/all_to_all | solution.py:50
  70.2 3.4 %factor.1.left = bf16[288,192]{1,0:T(8,128)(2,1)S(1)} custom-call(f32[32,256]{1,0:T(8,128)S(1)} %reshape.25.p), custom_call_target="tpu_custom_call" | custom-call | flops 4000000000 | tf_op jit(solution)/shard_map/factor/pallas_call | solution.py:214
  73.5 2.8 %all-to-all-done.4 = f32[32,1,2304]{2,1,0:T(1,128)S(1)} async-done(((f32[32,1,2304]{2,1,0:T(1,128)}), f32[32,1,2304]{2,1,0:T(1,128)S(1)}, u32[]{:S(2)}, u32[]{:S(2)}) %all-to-all-start.4) | async-done | bytes 294944 | tf_op jit(solution)/shard_map/all_to_all | solution.py:50
  76.4 1.4 %finish.1 = (bf16[256,2304]{1,0:T(8,128)(2,1)}, f32[32,2304]{1,0:T(8,128)}) custom-call(f32[576,128]{1,0:T(8,128)S(1)} %bitcast.13, bf16[288,192]{1,0:T(8,128)(2,1)S(1)} %factor.1.left), custom_call_target="tpu_custom_call" | custom-call | tf_op jit(solution)/shard_map/finish/pallas_call | solution.py:232
  (6 shorter events, 0.2 us)
Async XLA Ops:
  60.2 16.2 %all-to-all-start.4 = ((f32[32,1,2304]{2,1,0:T(1,128)}), f32[32,1,2304]{2,1,0:T(1,128)S(1)}, u32[]{:S(2)}, u32[]{:S(2)}) async-start(f32[32,1,2304]{2,1,0:T(1,128)} %bitcast.6), calls=%async_computation.4 | async-start | bytes 589824 | tf_op jit(solution)/shard_map/all_to_all | solution.py:50

commit v10 on v8

--- a/solution.py
+++ b/solution.py
@@ -211,6 +211,7 @@
         name="partial",
     )(in_vmem(p), in_vmem(corrected))
     raw = exchange(raw.reshape(PEERS, 1, COLS), ALONG_DP, FIRST_SCATTER, far=True)
+    raw, p = lax.optimization_barrier((raw, p))
     left = pl.pallas_call(
         factor,
         out_shape=pltpu.VMEM((ROWS + RANK, 6 * RANK), BF16),
@@ -220,7 +221,6 @@
         cost_estimate=pl.CostEstimate(flops=4_000_000_000, bytes_accessed=0, transcendentals=0),
         name="factor",
     )(in_vmem(p))
-    raw, left = lax.optimization_barrier((raw, left))
     raw = pl.pallas_call(
         gathered,
         out_shape=pltpu.VMEM(LINEAR, F32),

time: 78.1 us -> 78.1 us (level)
  waiting for transfers between devices: 4.72 us -> 2.84 us
  blocking collectives: 54.6 us -> 56.1 us
    all_to_all x1, waiting for transfers between devices: 4.72 us -> 2.84 us  [exchange(): lax.all_to_all(x, BOTH, 0, 0, axis_index_groups=groups_along(bits, first,...]
    all_to_all x4, blocking collectives: 54.6 us -> 56.1 us  [exchange(): lax.all_to_all(x, BOTH, 0, 0, axis_index_groups=groups_along(bits, first,...]
where the time goes in v10:
time: 78.1 us; the launch traced here: 77.7 us
  blocking collectives  56.1 us (72%)
  starting transfers between devices  9.96 us (13%)
  Pallas kernels  8 us (10%)
  waiting for transfers between devices  2.84 us (4%)
    all_to_all x4, blocking collectives, exchange(): lax.all_to_all(x, BOTH, 0, 0, axis_index_groups=groups_along(bits, first,...  56.1 us
    all_to_all x1, starting transfers between devices, exchange(): lax.all_to_all(x, BOTH, 0, 0, axis_index_groups=groups_along(bits, first,...  9.96 us
    pallas_call x1, Pallas kernels, local(): pl.pallas_call(factor, out_shape=pltpu.VMEM((ROWS + RANK, 6 * RANK), BF16...  3.36 us
    all_to_all x1, waiting for transfers between devices, exchange(): lax.all_to_all(x, BOTH, 0, 0, axis_index_groups=groups_along(bits, first,...  2.84 us
    pallas_call x1, Pallas kernels, local(): pl.pallas_call(project, out_shape=(pltpu.VMEM((RANK, ROWS), F32), pltpu.V...  2.17 us
  transfers between devices with their start and end apart: 1, of which 1 were waited for; matrix products, arithmetic and copies ran while one was open for 0% of the time, Pallas kernels for 4%

profile of v10, /device:TPU:40, one launch (start us, length us, event | category | flops | bytes accessed | tf_op | source)
XLA Modules:
  0.0 77.7 jit_solution(1939502451707176039)
XLA Ops:
  0.6 2.2 %project.1 = (f32[32,256]{1,0:T(8,128)S(1)}, bf16[256,2304]{1,0:T(8,128)(2,1)S(1)}) custom-call(bf16[256,2304]{1,0:T(8,128)(2,1)} %bitcast.16, bf16[256,2304]{1,0:T(8,128)(2,1)} %bitcast.17, f32[32,2304]{1,0:T(8,128)} %bitcast.18), custom_call_target="tpu_custom_call" | custom-call | tf_op jit(solution)/shard_map/project/pallas_call | solution.py:190
  2.8 9.2 %all_to_all.25 = f32[16,2,256]{2,1,0:T(2,128)S(1)} all-to-all(f32[16,2,256]{2,1,0:T(2,128)S(1)} %reshape.24), channel_id=1, replica_groups={{35,34,19,33,51,18,32,50,3,17,49,2,16,48,1,0},{39,38,23,37,55,22,36,54,..., dimensions={0} | all-to-all | bytes 65536 | tf_op jit(solution)/shard_map/all_to_all | solution.py:51
  12.0 21.1 %all_to_all.26 = f32[32,2,256]{2,1,0:T(2,128)S(1)} all-to-all(f32[32,2,256]{2,1,0:T(2,128)S(1)} %broadcast_in_dim.8), channel_id=1, replica_groups={{392,128,64,192,0,132,140,256,68,76,196,204,320,448,4,12,136,260,268,38..., dimensions={0} | all-to-all | bytes 131072 | tf_op jit(solution)/shard_map/all_to_all | solution.py:51
  33.2 8.4 %all_to_all.27 = f32[16,2,256]{2,1,0:T(2,128)S(1)} all-to-all(f32[16,2,256]{2,1,0:T(2,128)S(1)} %broadcast_in_dim.9), channel_id=1, replica_groups={{35,34,19,33,51,18,32,50,3,17,49,2,16,48,1,0},{39,38,23,37,55,22,36,54,..., dimensions={0} | all-to-all | bytes 65536 | tf_op jit(solution)/shard_map/all_to_all | solution.py:51
  41.6 0.3 partial.1
  42.0 17.4 %all_to_all.28 = f32[32,1,2304]{2,1,0:T(1,128)S(1)} all-to-all(f32[32,1,2304]{2,1,0:T(1,128)S(1)} %bitcast.15), channel_id=1, replica_groups={{352,64,0,80,112,128,16,48,96,144,176,192,448,32,160,208,240,256,384,46..., dimensions={0} | all-to-all | bytes 589824 | tf_op jit(solution)/shard_map/all_to_all | solution.py:51
  59.4 0.8 gathered.1
  60.1 10.0 %all-to-all-start.4 = ((f32[32,1,2304]{2,1,0:T(1,128)}), f32[32,1,2304]{2,1,0:T(1,128)S(1)}, u32[]{:S(2)}, u32[]{:S(2)}) async-start(f32[32,1,2304]{2,1,0:T(1,128)} %bitcast.6), calls=%async_computation.4 | async-start | bytes 589824 | tf_op jit(solution)/shard_map/all_to_all | solution.py:51
  70.1 3.4 %factor.1.left = bf16[288,192]{1,0:T(8,128)(2,1)S(1)} custom-call(f32[32,256]{1,0:T(8,128)S(1)} %reshape.25.p), custom_call_target="tpu_custom_call" | custom-call | flops 4000000000 | tf_op jit(solution)/shard_map/factor/pallas_call | solution.py:215
  73.5 2.8 %all-to-all-done.4 = f32[32,1,2304]{2,1,0:T(1,128)S(1)} async-done(((f32[32,1,2304]{2,1,0:T(1,128)}), f32[32,1,2304]{2,1,0:T(1,128)S(1)}, u32[]{:S(2)}, u32[]{:S(2)}) %all-to-all-start.4) | async-done | bytes 294944 | tf_op jit(solution)/shard_map/all_to_all | solution.py:51
  76.3 1.4 %finish.1 = (bf16[256,2304]{1,0:T(8,128)(2,1)}, f32[32,2304]{1,0:T(8,128)}) custom-call(f32[576,128]{1,0:T(8,128)S(1)} %bitcast.13, bf16[288,192]{1,0:T(8,128)(2,1)S(1)} %factor.1.left), custom_call_target="tpu_custom_call" | custom-call | tf_op jit(solution)/shard_map/finish/pallas_call | solution.py:233
  (6 shorter events, 0.2 us)
Async XLA Ops:
  60.1 16.2 %all-to-all-start.4 = ((f32[32,1,2304]{2,1,0:T(1,128)}), f32[32,1,2304]{2,1,0:T(1,128)S(1)}, u32[]{:S(2)}, u32[]{:S(2)}) async-start(f32[32,1,2304]{2,1,0:T(1,128)} %bitcast.6), calls=%async_computation.4 | async-start | bytes 589824 | tf_op jit(solution)/shard_map/all_to_all | solution.py:51
